TPU v7x, 512 devices: a whole 4x4x16 slice. The times are simulated.
512 devices in a mesh: row: 32 (over x, y, core), col: 16 (over z).
Axes of the slice: x: 4, y: 4, z: 16, core: 2. Of those that a mesh axis runs over, the one named last changes fastest.
Arguments:
- matrix: float32 [12800, 12800], P('row', 'col'), may hold values from -1.1 to 1.2, as said below
Outputs:
- swept: float32 [12800, 12800], P('row', 'col')
Inputs may be any that keep to these rules, and one draw needn't show every extreme that they name: `matrix`: exactly symmetric and positive definite.
All inputs are finite; a program needn't handle non-finite values.
Results may differ from a plain program's by a relative error of at most 0.00018.
Values sent between devices are 32-bit elements; how exact they have to be, the bound alone decides.
No kernel may reach another device: no remote copies, remote signals or barrier semaphores. Data moves between devices by JAX's collectives and lax.ppermute only.
A program may use at most 64 MiB of HBM per device.

v0:
```python
import functools

import jax
import jax.numpy as jnp
from jax import lax
from jax.experimental import pallas as pl
from jax.experimental.pallas import tpu as pltpu
from jax.sharding import Mesh
from jax.sharding import PartitionSpec as P

B = 384
K = 2
F32 = jnp.float32
HIGHEST = lax.Precision.HIGHEST
TILE = 128


def lane_splat(tile, lane):
    return jnp.broadcast_to(tile[:, lane : lane + 1], (8, TILE))


def row_splat(tile, row):
    return jnp.broadcast_to(tile[row : row + 1, :], (8, TILE))


def solve_eight(pivot, right):
    size = 8
    pivot = [list(row) for row in pivot]
    right = list(right)
    factor = [[None] * size for _ in range(size)]
    scale = [None] * size
    for j in range(size):
        recip = 1.0 / pivot[j][j]
        scale[j] = recip
        for m in range(j + 1, size):
            factor[m][j] = pivot[m][j] * recip
        for m in range(j + 1, size):
            for q in range(j + 1, m + 1):
                pivot[m][q] = pivot[m][q] - (pivot[m][j] * pivot[q][j]) * recip
            right[m] = right[m] - factor[m][j] * right[j]
    for j in range(size):
        right[j] = right[j] * scale[j]
    for j in reversed(range(size)):
        for m in range(j):
            right[m] = right[m] - factor[j][m] * right[j]
    return right


def invert_tile(rows):
    lane = lax.broadcasted_iota(jnp.int32, (8, TILE), 1)
    sub = lax.broadcasted_iota(jnp.int32, (8, TILE), 0)
    groups = len(rows)
    rows = list(rows)
    for g in range(groups):
        first = 8 * g
        here = rows[g]
        inside = (lane >= first) & (lane < first + 8)
        columns = [lane_splat(here, first + j) for j in range(8)]
        pivot = [[row_splat(columns[j], i) for j in range(i + 1)] for i in range(8)]
        start = jnp.where(inside, jnp.where(lane == first + sub, 1.0, 0.0), here)
        solved = solve_eight(pivot, [row_splat(start, i) for i in range(8)])
        for step in range(1, groups):
            i = (g + step) % groups
            terms = [lane_splat(rows[i], first + j) * solved[j] for j in range(8)]
            while len(terms) > 1:
                terms = [terms[2 * q] + terms[2 * q + 1] for q in range(len(terms) // 2)]
            rows[i] = jnp.where(inside, 0.0, rows[i]) - terms[0]
        merged = solved[0]
        for j in range(1, 8):
            merged = jnp.where(sub == j, solved[j], merged)
        rows[g] = merged
    return rows


def inverse_kernel(core_ref, own_ref, other_ref, out_ref):
    pairs, band, order = own_ref.shape
    core = core_ref[0]
    for i in range(pairs):
        out_ref[pl.ds(pl.multiple_of((2 * i + core) * band, 8), band), :] = own_ref[i]
        out_ref[pl.ds(pl.multiple_of((2 * i + 1 - core) * band, 8), band), :] = other_ref[i]
    unit = lax.broadcasted_iota(jnp.int32, (TILE, TILE), 0) == lax.broadcasted_iota(
        jnp.int32, (TILE, TILE), 1
    )

    def step(k, carry):
        here = pl.ds(pl.multiple_of(k * TILE, TILE), TILE)
        rows = invert_tile([out_ref[here, here][8 * i : 8 * i + 8, :] for i in range(TILE // 8)])
        inverse = jnp.concatenate(rows, axis=0)
        column = out_ref[:, here]
        out_ref[:, here] = jnp.zeros((order, TILE), F32)
        out_ref[here, here] = jnp.where(unit, 1.0, 0.0)
        lifted = jnp.dot(inverse, out_ref[here, :], precision=HIGHEST, preferred_element_type=F32)
        out_ref[here, here] = jnp.zeros((TILE, TILE), F32)
        out_ref[...] = out_ref[...] - jnp.dot(
            column, lifted, precision=HIGHEST, preferred_element_type=F32
        )
        out_ref[here, :] = lifted
        return carry

    lax.fori_loop(0, order // TILE, step, 0)


def pivot_inverse(core, own, other):
    order = own.shape[2]
    vmem = pl.BlockSpec(memory_space=pltpu.VMEM)
    return pl.pallas_call(
        inverse_kernel,
        out_shape=jax.ShapeDtypeStruct((order, order), F32),
        in_specs=[pl.BlockSpec(memory_space=pltpu.SMEM), vmem, vmem],
        out_specs=vmem,
        compiler_params=pltpu.CompilerParams(vmem_limit_bytes=20 * 1024 * 1024),
        cost_estimate=pl.CostEstimate(
            flops=order, bytes_accessed=8 * order, transcendentals=0
        ),
        name="pivot_inverse",
    )(core, own, other)


def update_kernel(place_ref, current_ref, column_ref, row_ref, inverse_ref, out_ref, *, band):
    rows, cols = current_ref.shape
    order = inverse_ref.shape[0]
    span = rows
    my_rows = place_ref[0] * band
    my_cols = place_ref[1] * (cols // span) * band

    def iota(shape, axis):
        return lax.broadcasted_iota(jnp.int32, shape, axis)

    column = column_ref[...]
    shape = (rows, order)
    pick = jnp.where(iota(shape, 1) == iota(shape, 0) + my_rows, -1.0, 0.0)
    column = jnp.where(iota(shape, 0) < band, pick, column)
    scaled = jnp.dot(column, inverse_ref[...], precision=HIGHEST, preferred_element_type=F32)

    def strip_of(shape):
        at = iota(shape, 1)
        inside = at < band
        within = at
        for g in range(1, cols // span):
            past = at - g * span
            now = (past >= 0) & (past < band)
            inside = inside | now
            within = jnp.where(now, past + g * band, within)
        return inside, within

    shape = (order, cols)
    inside, within = strip_of(shape)
    pick = jnp.where(iota(shape, 0) == within + my_cols, -1.0, 0.0)
    row = jnp.where(inside, pick, row_ref[...])
    shape = (rows, cols)
    inside, _ = strip_of(shape)
    base = jnp.where(inside | (iota(shape, 0) < band), 0.0, current_ref[...])
    out_ref[...] = base - jnp.dot(scaled, row, precision=HIGHEST, preferred_element_type=F32)


def trailing_update(place, current, column, row, inverse, band):
    vmem = pl.BlockSpec(memory_space=pltpu.VMEM)
    rows, cols = current.shape
    order = inverse.shape[0]
    return pl.pallas_call(
        functools.partial(update_kernel, band=band),
        out_shape=jax.ShapeDtypeStruct(current.shape, F32),
        in_specs=[pl.BlockSpec(memory_space=pltpu.SMEM)] + [vmem] * 4,
        out_specs=vmem,
        compiler_params=pltpu.CompilerParams(vmem_limit_bytes=20 * 1024 * 1024),
        cost_estimate=pl.CostEstimate(
            flops=2 * rows * order * (cols + order), bytes_accessed=8 * rows * cols, transcendentals=0
        ),
        name="trailing_update",
    )(place, current, column, row, inverse)


def body(matrix):
    rows, cols = matrix.shape
    groups = cols // rows
    depth = lax.axis_size("z")
    chips = lax.axis_size("x") * lax.axis_size("y")
    band = K * B // (2 * chips)
    core = lax.axis_index("c")
    place = jnp.stack([lax.axis_index(("x", "y", "c")), lax.axis_index("z")]).astype(jnp.int32)
    strip = jnp.concatenate(
        [matrix[:, g * rows : g * rows + band] for g in range(groups)], axis=1
    )
    rowband = matrix[0:band, :]
    with jax.named_scope("pivot_z"):
        pivot = lax.all_to_all(
            jnp.broadcast_to(strip[0:band, :], (depth, band, groups * band)), "z", 0, 0
        )
    pivot = pivot.transpose(1, 0, 2).reshape(band, K * B)
    with jax.named_scope("pivot_xy"):
        own = lax.all_to_all(jnp.broadcast_to(pivot, (chips, band, K * B)), ("x", "y"), 0, 0)
    with jax.named_scope("pivot_core"):
        other = lax.ppermute(own, "c", [(0, 1), (1, 0)])
    with jax.named_scope("column_panel"):
        column = lax.all_gather(strip.T, "z", axis=0, tiled=True)
    rowband = lax.optimization_barrier((rowband, own))[0]
    with jax.named_scope("row_panel"):
        row = lax.all_to_all(
            jnp.broadcast_to(rowband, (2 * chips, band, cols)), ("x", "y", "c"), 0, 0
        )
    inverse = pivot_inverse(core.astype(jnp.int32)[None], own, other)
    column, row, inverse = lax.optimization_barrier((column, row, inverse))
    return trailing_update(
        place, matrix, column.T, row.reshape(K * B, cols), inverse, band
    )


def solution(mesh):
    split = Mesh(mesh.devices.reshape(4, 4, 2, 16), ("x", "y", "c", "z"))
    spec = P(("x", "y", "c"), "z")
    return jax.shard_map(body, mesh=split, in_specs=(spec,), out_specs=spec, check_vma=False)
```

profile of v0, /device:TPU:4, one launch (start us, length us, event | category | flops | bytes accessed | tf_op | source)
XLA Modules:
  0.0 161.2 jit_solution(9738414451618407569)
XLA Ops:
  6.5 1.1 fusion.2
  7.7 0.1 copy.11
  7.8 0.1 copy.12
  7.9 0.1 copy.8
  8.0 0.2 reshape.8
  8.2 28.1 %all_to_all.15 = f32[16,1,1152]{2,1,0:T(1,128)S(1)} all-to-all(f32[16,1,1152]{2,1,0:T(1,128)S(1)} %reshape.8), channel_id=1, replica_groups=mesh['x'=4,'y'=4,'c'=2,'z'=16] {'z'}, dimensions={0} | all-to-all | bytes 147456 | tf_op jit(solution)/shard_map/pivot_z/all_to_all | solution.py:186
  36.3 0.5 broadcast
  36.8 0.8 reduce
  37.6 0.1 reshape.9
  37.8 0.1 reshape.6
  37.9 1.1 broadcast_in_dim.13
  39.0 0.0 slice-start
  39.0 7.6 %all-to-all-start.1 = ((f32[16,24,768]{2,1,0:T(8,128)}), f32[16,24,768]{2,1,0:T(8,128)S(1)}, u32[]{:S(2)}, u32[]{:S(2)}) async-start(f32[16,24,768]{2,1,0:T(8,128)} %broadcast_in_dim.13), calls=%async_computation.1 | async-start | bytes 2359296 | tf_op jit(solution)/shard_map/pivot_xy/all_to_all | solution.py:191
  46.6 14.6 %all-to-all-done.1.own_ref = f32[16,24,768]{2,1,0:T(8,128)S(1)} async-done(((f32[16,24,768]{2,1,0:T(8,128)}), f32[16,24,768]{2,1,0:T(8,128)S(1)}, u32[]{:S(2)}, u32[]{:S(2)}) %all-to-all-start.1) | async-done | bytes 1179680 | tf_op jit(solution)/shard_map/pivot_xy/all_to_all | solution.py:191
  61.1 0.0 slice-done
  61.1 0.0 copy-start.3
  61.1 1.9 %broadcast_in_dim.14 = f32[32,24,800]{2,1,0:T(8,128)} broadcast(f32[24,800]{1,0:T(8,128)S(1)} %slice-done), dimensions={1,2} | broadcast | bytes 2534400 | tf_op jit(solution)/shard_map/row_panel/broadcast_in_dim | solution.py:199
  63.0 0.1 copy-done.3
  63.1 6.2 %all-to-all-start.2 = ((f32[32,24,800]{2,1,0:T(8,128)}), f32[32,24,800]{2,1,0:T(8,128)S(1)}, u32[]{:S(2)}, u32[]{:S(2)}) async-start(f32[32,24,800]{2,1,0:T(8,128)} %broadcast_in_dim.14), calls=%async_computation.2 | async-start | bytes 5505024 | tf_op jit(solution)/shard_map/row_panel/all_to_all | solution.py:198
  69.3 0.0 all-gather.2.cloned.1.call-start
  69.4 0.7 fusion
  70.0 0.0 all-gather.2.cloned.1.call-update
  70.1 2.1 %collective-permute-start = (f32[16,24,768]{2,1,0:T(8,128)}, f32[16,24,768]{2,1,0:T(8,128)}, u32[]{:S(2)}, u32[]{:S(2)}) collective-permute-start(f32[16,24,768]{2,1,0:T(8,128)} %copy-done.3), channel_id=1, source_target_pairs={{0,16},{16,0},{1,17},{17,1},{2,18},{18,2},{3,19},{19,3},{4,20},{20... | collective-permute-start | bytes 3538952 | tf_op jit(solution)/shard_map/pivot_core/ppermute | solution.py:193
  72.1 0.1 pad_add_fusion.place_ref
  72.2 2.9 %collective-permute-done.other_ref = f32[16,24,768]{2,1,0:T(8,128)} collective-permute-done((f32[16,24,768]{2,1,0:T(8,128)}, f32[16,24,768]{2,1,0:T(8,128)}, u32[]{:S(2)}, u32[]{:S(2)}) %collective-permute-start) | collective-permute-done | bytes 1179680 | tf_op jit(solution)/shard_map/pivot_core/ppermute | solution.py:193
  75.1 0.0 copy-start.4
  75.1 1.3 copy-done.4
  76.4 50.6 %pivot_inverse.1.inverse_ref = f32[768,768]{1,0:T(8,128)S(1)} custom-call(s32[1]{0:T(128)} %bitcast.4.core_ref, f32[16,24,768]{2,1,0:T(8,128)S(1)} %copy-done.4, f32[16,24,768]{2,1,0:T(8,128)} %collective-permute-done.other_ref), custom_call_target="tpu_custom_call" | custom-call | flops 768 | bytes 6144 | tf_op jit(solution)/shard_map/pivot_inverse/pallas_call | solution.py:106
  127.0 0.0 copy-start
  127.0 1.4 copy-done
  128.4 10.1 %all-gather.2.cloned.1.call-done = f32[768,400]{1,0:T(8,128)} async-done(((f32[48,400]{1,0:T(8,128)}), f32[768,400]{1,0:T(8,128)}) %all-gather.2.cloned.1.call-update) | async-done | bytes 1228816 | tf_op jit(solution)/shard_map/column_panel/all_gather | solution.py:195
  138.5 0.0 all-to-all-done.2
  138.5 2.9 %copy.10 = f32[768,400]{0,1:T(8,128)} copy(f32[768,400]{1,0:T(8,128)} %all-gather.2.cloned.1.call-done) | data formatting | bytes 2457600 | tf_op jit(solution)/shard_map/optimization_barrier | solution.py:202
  141.4 0.0 copy-start.1
  141.4 1.7 %copy-done.1 = f32[768,768]{1,0:T(8,128)S(1)} copy-done((f32[768,768]{1,0:T(8,128)S(1)}, f32[768,768]{1,0:T(8,128)}, u32[]{:S(2)}) %copy-start.1) | copy-done | bytes 2359320
  143.1 0.0 copy-start.2
  143.1 1.3 copy-done.2
  144.3 0.0 copy-start.5
  144.3 1.4 copy-done.5
  145.7 8.7 %trailing_update.1 = f32[400,800]{1,0:T(8,128)} custom-call(s32[2]{0:T(128)S(1)} %pad_add_fusion.place_ref, f32[400,800]{1,0:T(8,128)S(1)} %copy-done.5, f32[400,768]{1,0:T(8,128)S(1)} %bitcast.9, f32[768,800]{1,0:T(8,128)S(1)} %bitcast.8, f32[768,768]{1,0:T(8,128)S(1)} %copy-done.1), custom_call_target="tpu_custom_call" | custom-call | flops 963379200 | bytes 2560000 | tf_op jit(solution)/shard_map/trailing_update/pallas_call | solution.py:160
  (3 shorter events, 0.1 us)
Async XLA Ops:
  39.0 22.1 %slice-start = ((f32[400,800]{1,0:T(8,128)}), f32[24,800]{1,0:T(8,128)S(1)}, s32[]{:S(2)}) async-start(f32[400,800]{1,0:T(8,128)} %current_ref.1), calls=%async_computation.4 | async-start | bytes 172032 | tf_op jit(solution)/shard_map/slice | solution.py:184
  39.0 22.1 %all-to-all-start.1 = ((f32[16,24,768]{2,1,0:T(8,128)}), f32[16,24,768]{2,1,0:T(8,128)S(1)}, u32[]{:S(2)}, u32[]{:S(2)}) async-start(f32[16,24,768]{2,1,0:T(8,128)} %broadcast_in_dim.13), calls=%async_computation.1 | async-start | bytes 2359296 | tf_op jit(solution)/shard_map/pivot_xy/all_to_all | solution.py:191
  61.1 1.9 %copy-start.3 = (f32[16,24,768]{2,1,0:T(8,128)}, f32[16,24,768]{2,1,0:T(8,128)S(1)}, u32[]{:S(2)}) copy-start(f32[16,24,768]{2,1,0:T(8,128)S(1)} %all-to-all-done.1.own_ref) | copy-start | bytes 3538948
  63.1 75.5 %all-to-all-start.2 = ((f32[32,24,800]{2,1,0:T(8,128)}), f32[32,24,800]{2,1,0:T(8,128)S(1)}, u32[]{:S(2)}, u32[]{:S(2)}) async-start(f32[32,24,800]{2,1,0:T(8,128)} %broadcast_in_dim.14), calls=%async_computation.2 | async-start | bytes 5505024 | tf_op jit(solution)/shard_map/row_panel/all_to_all | solution.py:198
  69.3 69.2 %all-gather.2.cloned.1.call-start = ((), (), s32[]{:S(2)}) async-start(), calls=%async_computation.3 | async-start | bytes 1671168 | tf_op jit(solution)/shard_map/column_panel/all_gather | solution.py:195
  70.1 5.1 %collective-permute-start = (f32[16,24,768]{2,1,0:T(8,128)}, f32[16,24,768]{2,1,0:T(8,128)}, u32[]{:S(2)}, u32[]{:S(2)}) collective-permute-start(f32[16,24,768]{2,1,0:T(8,128)} %copy-done.3), channel_id=1, source_target_pairs={{0,16},{16,0},{1,17},{17,1},{2,18},{18,2},{3,19},{19,3},{4,20},{20... | collective-permute-start | bytes 3538952 | tf_op jit(solution)/shard_map/pivot_core/ppermute | solution.py:193
  75.1 1.3 copy-start.4
  127.0 1.4 copy-start
  141.4 1.7 %copy-start.1 = (f32[768,768]{1,0:T(8,128)S(1)}, f32[768,768]{1,0:T(8,128)}, u32[]{:S(2)}) copy-start(f32[768,768]{1,0:T(8,128)} %copy-done) | copy-start | bytes 7077892
  143.1 1.3 copy-start.2
  144.3 1.4 copy-start.5
Sparse Core Ops, SparseCore 0:
  72.2 66.2 all-gather.1
where the time goes:
time: 162 us; the launch traced here: 161 us
  Pallas kernels  59.2 us (37%)
  blocking collectives  28.1 us (17%)
  waiting for transfers between devices  27.6 us (17%)
  starting transfers between devices  15.9 us (10%)
  local copies, waits for them, and re-layouts  15.3 us (9%)
  between operations  13.5 us (8%)
    pallas_call x1, Pallas kernels, pivot_inverse(): pl.pallas_call(inverse_kernel, out_shape=jax.ShapeDtypeStruct((order, ord...  50.6 us
    all_to_all x1, blocking collectives, body(): lax.all_to_all(jnp.broadcast_to(strip[0:band, :], (depth, band, groups *...  28.1 us
    all_to_all x1, waiting for transfers between devices, body(): lax.all_to_all(jnp.broadcast_to(pivot, (chips, band, K * B)), ('x', 'y'),...  14.6 us
    all_gather x1, waiting for transfers between devices, body(): column = lax.all_gather(strip.T, 'z', axis=0, tiled=True)  10.1 us
    pallas_call x1, Pallas kernels, trailing_update(): pl.pallas_call(functools.partial(update_kernel, band=band), out_shape=jax...  8.67 us
    unnamed x16, local copies, waits for them, and re-layouts  7.6 us
    all_to_all x1, starting transfers between devices, body(): lax.all_to_all(jnp.broadcast_to(pivot, (chips, band, K * B)), ('x', 'y'),...  7.58 us
    all_to_all x1, starting transfers between devices, body(): lax.all_to_all(jnp.broadcast_to(rowband, (2 * chips, band, cols)), ('x',...  6.25 us
  transfers between devices with their start and end apart: 4, of which 3 were waited for; matrix products, arithmetic and copies ran while one was open for 0% of the time, Pallas kernels for 31%

commit v1 on v0

--- a/solution.py
+++ b/solution.py
@@ -11,6 +11,7 @@
 B = 384
 K = 2
 F32 = jnp.float32
+BF16 = jnp.bfloat16
 HIGHEST = lax.Precision.HIGHEST
 TILE = 128
 
@@ -72,8 +73,30 @@
     return rows
 
 
-def inverse_kernel(core_ref, own_ref, other_ref, out_ref):
+def three_parts(value):
+    high = value.astype(BF16)
+    rest = value - high.astype(F32)
+    middle = rest.astype(BF16)
+    return high, middle, (rest - middle.astype(F32)).astype(BF16)
+
+
+def left_parts(value):
+    high, middle, low = three_parts(value)
+    return jnp.concatenate([high, high, middle, high, low, middle], axis=1)
+
+
+def right_parts(value):
+    high, middle, low = three_parts(value)
+    return jnp.concatenate([high, middle, high, low, high, middle], axis=0)
+
+
+def product(left, right):
+    return jnp.dot(left, right, preferred_element_type=F32)
+
+
+def inverse_kernel(core_ref, own_ref, other_ref, out_ref, left_ref, right_ref, diagonal_ref):
     pairs, band, order = own_ref.shape
+    blocks = order // TILE
     core = core_ref[0]
     for i in range(pairs):
         out_ref[pl.ds(pl.multiple_of((2 * i + core) * band, 8), band), :] = own_ref[i]
@@ -81,23 +104,36 @@
     unit = lax.broadcasted_iota(jnp.int32, (TILE, TILE), 0) == lax.broadcasted_iota(
         jnp.int32, (TILE, TILE), 1
     )
+    unit = jnp.where(unit, 1.0, 0.0)
+    diagonal_ref[...] = out_ref[0:TILE, 0:TILE]
+    left_ref[...] = jnp.zeros(left_ref.shape, BF16)
+    right_ref[...] = jnp.zeros(right_ref.shape, BF16)
+
+    def apply_last():
+        for c in range(blocks):
+            here = slice(TILE * c, TILE * c + TILE)
+            out_ref[:, here] = out_ref[:, here] - product(left_ref[...], right_ref[:, here])
 
     def step(k, carry):
         here = pl.ds(pl.multiple_of(k * TILE, TILE), TILE)
-        rows = invert_tile([out_ref[here, here][8 * i : 8 * i + 8, :] for i in range(TILE // 8)])
+        apply_last()
+        block = diagonal_ref[...]
+        rows = invert_tile([block[8 * i : 8 * i + 8, :] for i in range(TILE // 8)])
         inverse = jnp.concatenate(rows, axis=0)
+        row = out_ref[here, :]
+        out_ref[here, here] = -unit
         column = out_ref[:, here]
         out_ref[:, here] = jnp.zeros((order, TILE), F32)
-        out_ref[here, here] = jnp.where(unit, 1.0, 0.0)
-        lifted = jnp.dot(inverse, out_ref[here, :], precision=HIGHEST, preferred_element_type=F32)
-        out_ref[here, here] = jnp.zeros((TILE, TILE), F32)
-        out_ref[...] = out_ref[...] - jnp.dot(
-            column, lifted, precision=HIGHEST, preferred_element_type=F32
-        )
-        out_ref[here, :] = lifted
+        left_ref[...] = left_parts(product(left_parts(column), right_parts(inverse)))
+        right_ref[...] = right_parts(row)
+        right_ref[:, here] = right_parts(unit)
+        out_ref[here, :] = jnp.zeros((TILE, order), F32)
+        after = pl.ds(pl.multiple_of(jnp.minimum(k + 1, blocks - 1) * TILE, TILE), TILE)
+        diagonal_ref[...] = out_ref[after, after] - product(left_ref[after, :], right_ref[:, after])
         return carry
 
-    lax.fori_loop(0, order // TILE, step, 0)
+    lax.fori_loop(0, blocks, step, 0)
+    apply_last()
 
 
 def pivot_inverse(core, own, other):
@@ -108,16 +144,21 @@
         out_shape=jax.ShapeDtypeStruct((order, order), F32),
         in_specs=[pl.BlockSpec(memory_space=pltpu.SMEM), vmem, vmem],
         out_specs=vmem,
+        scratch_shapes=[
+            pltpu.VMEM((order, 6 * TILE), BF16),
+            pltpu.VMEM((6 * TILE, order), BF16),
+            pltpu.VMEM((TILE, TILE), F32),
+        ],
         compiler_params=pltpu.CompilerParams(vmem_limit_bytes=20 * 1024 * 1024),
-        cost_estimate=pl.CostEstimate(
-            flops=order, bytes_accessed=8 * order, transcendentals=0
-        ),
+        cost_estimate=pl.CostEstimate(flops=1, bytes_accessed=8, transcendentals=0),
         name="pivot_inverse",
     )(core, own, other)
 
 
-def update_kernel(place_ref, current_ref, column_ref, row_ref, inverse_ref, out_ref, *, band):
-    rows, cols = current_ref.shape
+def update_kernel(place_ref, column_ref, row_ref, inverse_ref, current_ref, out_ref, held, sem, *, band):
+    copy = pltpu.make_async_copy(current_ref, held, sem)
+    copy.start()
+    rows, cols = held.shape
     order = inverse_ref.shape[0]
     span = rows
     my_rows = place_ref[0] * band
@@ -126,11 +167,10 @@
     def iota(shape, axis):
         return lax.broadcasted_iota(jnp.int32, shape, axis)
 
-    column = column_ref[...]
-    shape = (rows, order)
-    pick = jnp.where(iota(shape, 1) == iota(shape, 0) + my_rows, -1.0, 0.0)
-    column = jnp.where(iota(shape, 0) < band, pick, column)
-    scaled = jnp.dot(column, inverse_ref[...], precision=HIGHEST, preferred_element_type=F32)
+    shape = (order, rows)
+    pick = jnp.where(iota(shape, 0) == iota(shape, 1) + my_rows, -1.0, 0.0)
+    column = jnp.where(iota(shape, 1) < band, pick, column_ref[...])
+    scaled = jnp.dot(inverse_ref[...], column, precision=HIGHEST, preferred_element_type=F32).T
 
     def strip_of(shape):
         at = iota(shape, 1)
@@ -149,8 +189,14 @@
     row = jnp.where(inside, pick, row_ref[...])
     shape = (rows, cols)
     inside, _ = strip_of(shape)
-    base = jnp.where(inside | (iota(shape, 0) < band), 0.0, current_ref[...])
-    out_ref[...] = base - jnp.dot(scaled, row, precision=HIGHEST, preferred_element_type=F32)
+    scaled_high, scaled_low, _ = three_parts(scaled)
+    row_high, row_low, _ = three_parts(row)
+    change = product(scaled_high, row_high) + (
+        product(scaled_high, row_low) + product(scaled_low, row_high)
+    )
+    copy.wait()
+    base = jnp.where(inside | (iota(shape, 0) < band), 0.0, held[...])
+    out_ref[...] = base - change
 
 
 def trailing_update(place, current, column, row, inverse, band):
@@ -160,14 +206,17 @@
     return pl.pallas_call(
         functools.partial(update_kernel, band=band),
         out_shape=jax.ShapeDtypeStruct(current.shape, F32),
-        in_specs=[pl.BlockSpec(memory_space=pltpu.SMEM)] + [vmem] * 4,
+        in_specs=[pl.BlockSpec(memory_space=pltpu.SMEM)]
+        + [vmem] * 3
+        + [pl.BlockSpec(memory_space=pl.ANY)],
         out_specs=vmem,
+        scratch_shapes=[pltpu.VMEM(current.shape, F32), pltpu.SemaphoreType.DMA(())],
         compiler_params=pltpu.CompilerParams(vmem_limit_bytes=20 * 1024 * 1024),
         cost_estimate=pl.CostEstimate(
             flops=2 * rows * order * (cols + order), bytes_accessed=8 * rows * cols, transcendentals=0
         ),
         name="trailing_update",
-    )(place, current, column, row, inverse)
+    )(place, column, row, inverse, current)
 
 
 def body(matrix):
@@ -193,15 +242,12 @@
         other = lax.ppermute(own, "c", [(0, 1), (1, 0)])
     with jax.named_scope("column_panel"):
         column = lax.all_gather(strip.T, "z", axis=0, tiled=True)
-    rowband = lax.optimization_barrier((rowband, own))[0]
     with jax.named_scope("row_panel"):
-        row = lax.all_to_all(
-            jnp.broadcast_to(rowband, (2 * chips, band, cols)), ("x", "y", "c"), 0, 0
-        )
+        row = lax.all_gather(rowband, ("x", "y", "c"), axis=0, tiled=True)
     inverse = pivot_inverse(core.astype(jnp.int32)[None], own, other)
     column, row, inverse = lax.optimization_barrier((column, row, inverse))
     return trailing_update(
-        place, matrix, column.T, row.reshape(K * B, cols), inverse, band
+        place, matrix, column, row.reshape(K * B, cols), inverse, band
     )
 
 

time: 162 us -> 167 us (1.031)
  the two profiles are of different devices: /device:TPU:4 before, /device:TPU:1 now
where the time goes in v1:
time: 167 us
  blocking collectives  49.5 us (30%)
  Pallas kernels  47.5 us (28%)
  waiting for transfers between devices  38.4 us (23%)
  between operations  13.5 us (8%)
  local copies, waits for them, and re-layouts  10.9 us (7%)
  starting transfers between devices  5.66 us (3%)
    pallas_call x1, Pallas kernels, pivot_inverse(): pl.pallas_call(inverse_kernel, out_shape=jax.ShapeDtypeStruct((order, ord...  39.5 us
    all_gather x1, waiting for transfers between devices, body(): row = lax.all_gather(rowband, ('x', 'y', 'c'), axis=0, tiled=True)  36 us
    all_to_all x1, blocking collectives, body(): lax.all_to_all(jnp.broadcast_to(strip[0:band, :], (depth, band, groups *...  27.3 us
    all_to_all x1, blocking collectives, body(): lax.all_to_all(jnp.broadcast_to(pivot, (chips, band, K * B)), ('x', 'y'),...  22.2 us
    pallas_call x1, Pallas kernels, trailing_update(): pl.pallas_call(functools.partial(update_kernel, band=band), out_shape=jax...  8.05 us
    unnamed x14, local copies, waits for them, and re-layouts  7.36 us
    ppermute x1, starting transfers between devices, body(): other = lax.ppermute(own, 'c', [(0, 1), (1, 0)])  5.62 us
  transfers between devices with their start and end apart: 3, of which 2 were waited for; matrix products, arithmetic and copies ran while one was open for 2% of the time, Pallas kernels for 24%

profile of v1, /device:TPU:1, one launch (start us, length us, event | category | flops | bytes accessed | tf_op | source)
XLA Modules:
  0.0 167.0 jit_solution(7303645781178362576)
XLA Ops:
  6.5 0.0 all-gather.3.cloned.1.call-start
  6.5 1.1 fusion.2
  7.7 0.1 copy.12
  7.8 0.1 copy.13
  7.9 0.7 fusion
  8.6 0.0 all-gather.3.cloned.1.call-update
  8.6 0.0 all-gather.5.cloned.1.call-start
  8.6 1.5 slice.14
  10.2 0.0 all-gather.5.cloned.1.call-update
  10.2 0.1 copy.10
  10.3 0.2 reshape.4
  10.5 27.3 %all_to_all.10 = f32[16,1,1152]{2,1,0:T(1,128)S(1)} all-to-all(f32[16,1,1152]{2,1,0:T(1,128)S(1)} %reshape.4), channel_id=1, replica_groups=mesh['x'=4,'y'=4,'c'=2,'z'=16] {'z'}, dimensions={0} | all-to-all | bytes 147456 | tf_op jit(solution)/shard_map/pivot_z/all_to_all | solution.py:235
  37.7 0.5 broadcast
  38.3 0.8 reduce
  39.1 0.1 reshape.5
  39.3 0.1 reshape.3
  39.4 0.1 broadcast_in_dim.11
  39.5 22.2 %all_to_all.11.own_ref = f32[16,24,768]{2,1,0:T(8,128)S(1)} all-to-all(f32[16,24,768]{2,1,0:T(8,128)S(1)} %broadcast_in_dim.11), channel_id=1, replica_groups=mesh['x'=4,'y'=4,'c'=2,'z'=16] {'x','y'}, dimensions={0} | all-to-all | bytes 2359296 | tf_op jit(solution)/shard_map/pivot_xy/all_to_all | solution.py:240
  61.7 5.6 %collective-permute-start = (f32[16,24,768]{2,1,0:T(8,128)S(1)}, f32[16,24,768]{2,1,0:T(8,128)S(1)}, u32[]{:S(2)}, u32[]{:S(2)}) collective-permute-start(f32[16,24,768]{2,1,0:T(8,128)S(1)} %all_to_all.11.own_ref), channel_id=1, source_target_pairs={{0,16},{16,0},{1,17},{17,1},{2,18},{18,2},{3,19},{19,3},{4,20},{20... | collective-permute-start | bytes 3538952 | tf_op jit(solution)/shard_map/pivot_core/ppermute | solution.py:242
  67.3 0.1 pad_add_fusion.place_ref
  67.4 2.4 %collective-permute-done.other_ref = f32[16,24,768]{2,1,0:T(8,128)S(1)} collective-permute-done((f32[16,24,768]{2,1,0:T(8,128)S(1)}, f32[16,24,768]{2,1,0:T(8,128)S(1)}, u32[]{:S(2)}, u32[]{:S(2)}) %collective-permute-start) | collective-permute-done | bytes 1179680 | tf_op jit(solution)/shard_map/pivot_core/ppermute | solution.py:242
  69.8 0.0 copy-start.3
  69.8 1.0 copy-done.3
  70.8 0.0 copy-start.4
  70.8 1.3 copy-done.4
  72.1 39.5 %pivot_inverse.1.inverse_ref = f32[768,768]{1,0:T(8,128)S(1)} custom-call(s32[1]{0:T(128)} %bitcast.3.core_ref, f32[16,24,768]{2,1,0:T(8,128)S(1)} %all_to_all.11.own_ref, f32[16,24,768]{2,1,0:T(8,128)S(1)} %copy-done.4), custom_call_target="tpu_custom_call" | custom-call | flops 1 | bytes 8 | tf_op jit(solution)/shard_map/pivot_inverse/pallas_call | solution.py:142
  111.5 0.0 all-gather.3.cloned.1.call-done.column_ref
  111.6 36.0 %all-gather.5.cloned.1.call-done.row_ref = f32[768,800]{1,0:T(8,128)} async-done(((f32[24,800]{1,0:T(8,128)}), f32[768,800]{1,0:T(8,128)}) %all-gather.5.cloned.1.call-update) | async-done | bytes 2457616 | tf_op jit(solution)/shard_map/row_panel/all_gather | solution.py:246
  147.5 0.0 copy-start
  147.5 1.8 %copy-done = f32[768,800]{1,0:T(8,128)S(1)} copy-done((f32[768,800]{1,0:T(8,128)S(1)}, f32[768,800]{1,0:T(8,128)}, u32[]{:S(2)}) %copy-start) | copy-done | bytes 2457624
  149.3 0.0 copy-start.1
  149.3 1.4 copy-done.1
  150.7 0.0 copy-start.2
  150.7 1.4 copy-done.2
  152.1 8.1 %trailing_update.1 = f32[400,800]{1,0:T(8,128)} custom-call(s32[2]{0:T(128)S(1)} %pad_add_fusion.place_ref, f32[768,400]{1,0:T(8,128)S(1)} %copy-done.2, f32[768,800]{1,0:T(8,128)S(1)} %copy-done, f32[768,768]{1,0:T(8,128)S(1)} %pivot_inverse.1.inverse_ref, f32[400,800]{1,0:T(8,128)S(1)} %copy-done.1), custom_call_target="tpu_custom_call" | custom-call | flops 963379200 | bytes 2560000 | tf_op jit(solution)/shard_map/trailing_update/pallas_call | solution.py:206
  (3 shorter events, 0.1 us)
Async XLA Ops:
  6.5 105.0 %all-gather.3.cloned.1.call-start = ((), (), s32[]{:S(2)}) async-start(), calls=%async_computation.2 | async-start | bytes 1671168 | tf_op jit(solution)/shard_map/column_panel/all_gather | solution.py:244
  8.6 138.9 %all-gather.5.cloned.1.call-start = ((), (), s32[]{:S(2)}) async-start(), calls=%async_computation.3 | async-start | bytes 2838528 | tf_op jit(solution)/shard_map/row_panel/all_gather | solution.py:246
  61.7 8.1 %collective-permute-start = (f32[16,24,768]{2,1,0:T(8,128)S(1)}, f32[16,24,768]{2,1,0:T(8,128)S(1)}, u32[]{:S(2)}, u32[]{:S(2)}) collective-permute-start(f32[16,24,768]{2,1,0:T(8,128)S(1)} %all_to_all.11.own_ref), channel_id=1, source_target_pairs={{0,16},{16,0},{1,17},{17,1},{2,18},{18,2},{3,19},{19,3},{4,20},{20... | collective-permute-start | bytes 3538952 | tf_op jit(solution)/shard_map/pivot_core/ppermute | solution.py:242
  69.8 1.0 copy-start.3
  70.8 1.3 copy-start.4
  147.5 1.8 %copy-start = (f32[768,800]{1,0:T(8,128)S(1)}, f32[768,800]{1,0:T(8,128)}, u32[]{:S(2)}) copy-start(f32[768,800]{1,0:T(8,128)} %all-gather.5.cloned.1.call-done.row_ref) | copy-start | bytes 7372804
  149.3 1.4 copy-start.1
  150.7 1.4 copy-start.2
Sparse Core Ops, SparseCore 0:
  9.4 68.7 all-gather.2
  81.4 66.0 all-gather.4

commit v2 on v1

--- a/solution.py
+++ b/solution.py
@@ -94,13 +94,12 @@
     return jnp.dot(left, right, preferred_element_type=F32)
 
 
-def inverse_kernel(core_ref, own_ref, other_ref, out_ref, left_ref, right_ref, diagonal_ref):
+def inverse_kernel(slot_ref, own_ref, other_ref, out_ref, left_ref, right_ref, diagonal_ref):
     pairs, band, order = own_ref.shape
     blocks = order // TILE
-    core = core_ref[0]
     for i in range(pairs):
-        out_ref[pl.ds(pl.multiple_of((2 * i + core) * band, 8), band), :] = own_ref[i]
-        out_ref[pl.ds(pl.multiple_of((2 * i + 1 - core) * band, 8), band), :] = other_ref[i]
+        out_ref[pl.ds(pl.multiple_of(slot_ref[0, i] * band, 8), band), :] = own_ref[i]
+        out_ref[pl.ds(pl.multiple_of(slot_ref[1, i] * band, 8), band), :] = other_ref[i]
     unit = lax.broadcasted_iota(jnp.int32, (TILE, TILE), 0) == lax.broadcasted_iota(
         jnp.int32, (TILE, TILE), 1
     )
@@ -136,7 +135,7 @@
     apply_last()
 
 
-def pivot_inverse(core, own, other):
+def pivot_inverse(slots, own, other):
     order = own.shape[2]
     vmem = pl.BlockSpec(memory_space=pltpu.VMEM)
     return pl.pallas_call(
@@ -152,13 +151,22 @@
         compiler_params=pltpu.CompilerParams(vmem_limit_bytes=20 * 1024 * 1024),
         cost_estimate=pl.CostEstimate(flops=1, bytes_accessed=8, transcendentals=0),
         name="pivot_inverse",
-    )(core, own, other)
-
-
-def update_kernel(place_ref, column_ref, row_ref, inverse_ref, current_ref, out_ref, held, sem, *, band):
-    copy = pltpu.make_async_copy(current_ref, held, sem)
-    copy.start()
-    rows, cols = held.shape
+    )(slots, own, other)
+
+
+def update_kernel(
+    place_ref, column_hbm, inverse_hbm, row_hbm, current_hbm, out_ref,
+    column_ref, inverse_ref, row_ref, current_ref, sems, *, band,
+):
+    sources = (column_hbm, inverse_hbm, row_hbm, current_hbm)
+    targets = (column_ref, inverse_ref, row_ref, current_ref)
+    loads = [
+        pltpu.make_async_copy(source, target, sems.at[i])
+        for i, (source, target) in enumerate(zip(sources, targets))
+    ]
+    for load in loads:
+        load.start()
+    rows, cols = current_ref.shape
     order = inverse_ref.shape[0]
     span = rows
     my_rows = place_ref[0] * band
@@ -167,9 +175,11 @@
     def iota(shape, axis):
         return lax.broadcasted_iota(jnp.int32, shape, axis)
 
+    loads[0].wait()
     shape = (order, rows)
     pick = jnp.where(iota(shape, 0) == iota(shape, 1) + my_rows, -1.0, 0.0)
     column = jnp.where(iota(shape, 1) < band, pick, column_ref[...])
+    loads[1].wait()
     scaled = jnp.dot(inverse_ref[...], column, precision=HIGHEST, preferred_element_type=F32).T
 
     def strip_of(shape):
@@ -186,6 +196,7 @@
     shape = (order, cols)
     inside, within = strip_of(shape)
     pick = jnp.where(iota(shape, 0) == within + my_cols, -1.0, 0.0)
+    loads[2].wait()
     row = jnp.where(inside, pick, row_ref[...])
     shape = (rows, cols)
     inside, _ = strip_of(shape)
@@ -194,29 +205,33 @@
     change = product(scaled_high, row_high) + (
         product(scaled_high, row_low) + product(scaled_low, row_high)
     )
-    copy.wait()
-    base = jnp.where(inside | (iota(shape, 0) < band), 0.0, held[...])
+    loads[3].wait()
+    base = jnp.where(inside | (iota(shape, 0) < band), 0.0, current_ref[...])
     out_ref[...] = base - change
 
 
 def trailing_update(place, current, column, row, inverse, band):
-    vmem = pl.BlockSpec(memory_space=pltpu.VMEM)
     rows, cols = current.shape
     order = inverse.shape[0]
     return pl.pallas_call(
         functools.partial(update_kernel, band=band),
         out_shape=jax.ShapeDtypeStruct(current.shape, F32),
         in_specs=[pl.BlockSpec(memory_space=pltpu.SMEM)]
-        + [vmem] * 3
-        + [pl.BlockSpec(memory_space=pl.ANY)],
-        out_specs=vmem,
-        scratch_shapes=[pltpu.VMEM(current.shape, F32), pltpu.SemaphoreType.DMA(())],
-        compiler_params=pltpu.CompilerParams(vmem_limit_bytes=20 * 1024 * 1024),
+        + [pl.BlockSpec(memory_space=pl.ANY)] * 4,
+        out_specs=pl.BlockSpec(memory_space=pltpu.VMEM),
+        scratch_shapes=[
+            pltpu.VMEM(column.shape, F32),
+            pltpu.VMEM(inverse.shape, F32),
+            pltpu.VMEM(row.shape, F32),
+            pltpu.VMEM(current.shape, F32),
+            pltpu.SemaphoreType.DMA((4,)),
+        ],
+        compiler_params=pltpu.CompilerParams(vmem_limit_bytes=56 * 1024 * 1024),
         cost_estimate=pl.CostEstimate(
             flops=2 * rows * order * (cols + order), bytes_accessed=8 * rows * cols, transcendentals=0
         ),
         name="trailing_update",
-    )(place, column, row, inverse, current)
+    )(place, column, inverse, row, current)
 
 
 def body(matrix):
@@ -232,20 +247,29 @@
     )
     rowband = matrix[0:band, :]
     with jax.named_scope("pivot_z"):
-        pivot = lax.all_to_all(
-            jnp.broadcast_to(strip[0:band, :], (depth, band, groups * band)), "z", 0, 0
-        )
-    pivot = pivot.transpose(1, 0, 2).reshape(band, K * B)
-    with jax.named_scope("pivot_xy"):
-        own = lax.all_to_all(jnp.broadcast_to(pivot, (chips, band, K * B)), ("x", "y"), 0, 0)
+        pivot = lax.all_gather(strip[0:band, :], "z", axis=0, tiled=False)
+    own = pivot.transpose(1, 0, 2).reshape(1, band, K * B)
+    for axis in ("y", "x"):
+        size = lax.axis_size(axis)
+        with jax.named_scope("pivot_" + axis):
+            pieces = [own] + [
+                lax.ppermute(own, axis, [(i, (i + hop) % size) for i in range(size)])
+                for hop in range(1, size)
+            ]
+        own = jnp.concatenate(pieces, axis=0)
     with jax.named_scope("pivot_core"):
         other = lax.ppermute(own, "c", [(0, 1), (1, 0)])
     with jax.named_scope("column_panel"):
         column = lax.all_gather(strip.T, "z", axis=0, tiled=True)
+    spread = jnp.broadcast_to(rowband, (2 * chips, band, cols))
     with jax.named_scope("row_panel"):
-        row = lax.all_gather(rowband, ("x", "y", "c"), axis=0, tiled=True)
-    inverse = pivot_inverse(core.astype(jnp.int32)[None], own, other)
-    column, row, inverse = lax.optimization_barrier((column, row, inverse))
+        row = lax.all_to_all(spread, ("x", "y", "c"), 0, 0)
+    hops = jnp.arange(chips, dtype=jnp.int32)
+    size_x, size_y = lax.axis_size("x"), lax.axis_size("y")
+    from_x = (lax.axis_index("x") - hops // size_y) % size_x
+    from_y = (lax.axis_index("y") - hops % size_y) % size_y
+    first = 2 * (from_x * size_y + from_y)
+    inverse = pivot_inverse(jnp.stack([first + core, first + 1 - core]), own, other)
     return trailing_update(
         place, matrix, column, row.reshape(K * B, cols), inverse, band
     )

time: 167 us -> 152 us (0.910)
  starting transfers between devices: 5.66 us -> 39.3 us
  waiting for transfers between devices: 38.4 us -> 11.6 us
  blocking collectives: 49.5 us -> 30 us
  local copies, waits for them, and re-layouts: 10.9 us -> 4.87 us
  Pallas kernels: 47.5 us -> 51 us
    all_to_all x2 -> x0, blocking collectives: 49.5 us -> none  [the longest x1 27.3 us: body(): lax.all_to_all(jnp.broadcast_to(strip[0:band, :], (depth, band, groups *...]
    all_gather x1 -> x0, waiting for transfers between devices: 36 us -> none  [body(): row = lax.all_gather(rowband, ('x', 'y', 'c'), axis=0, tiled=True)]
    all_gather x0 -> x1, blocking collectives: none -> 30 us  [body(): pivot = lax.all_gather(strip[0:band, :], 'z', axis=0, tiled=False)]
    ppermute x0 -> x6, starting transfers between devices: none -> 19.3 us  [body(): lax.ppermute(own, axis, [(i, (i + hop) % size) for i in range(size)])]
    all_to_all x0 -> x1, starting transfers between devices: none -> 11.3 us  [body(): row = lax.all_to_all(spread, ('x', 'y', 'c'), 0, 0)]
    ppermute x0 -> x6, waiting for transfers between devices: none -> 9.8 us  [body(): lax.ppermute(own, axis, [(i, (i + hop) % size) for i in range(size)])]
    unnamed x14 -> x9, local copies, waits for them, and re-layouts: 7.36 us -> 1.67 us
    ppermute x1, starting transfers between devices: 5.62 us -> 8.72 us  [body(): other = lax.ppermute(own, 'c', [(0, 1), (1, 0)])]
  transfers between devices with their start and end apart: 3 -> 9, of which waited for: 2 -> 4; matrix products, arithmetic and copies ran while one was open for 2% -> 2% of each run, Pallas kernels for 24% -> 27%
where the time goes in v2:
time: 152 us
  Pallas kernels  51 us (34%)
  starting transfers between devices  39.3 us (26%)
  blocking collectives  30 us (20%)
  between operations  13.6 us (9%)
  waiting for transfers between devices  11.6 us (8%)
  local copies, waits for them, and re-layouts  4.87 us (3%)
    pallas_call x1, Pallas kernels, pivot_inverse(): pl.pallas_call(inverse_kernel, out_shape=jax.ShapeDtypeStruct((order, ord...  40.5 us
    all_gather x1, blocking collectives, body(): pivot = lax.all_gather(strip[0:band, :], 'z', axis=0, tiled=False)  30 us
    ppermute x6, starting transfers between devices, body(): lax.ppermute(own, axis, [(i, (i + hop) % size) for i in range(size)])  19.3 us
    all_to_all x1, starting transfers between devices, body(): row = lax.all_to_all(spread, ('x', 'y', 'c'), 0, 0)  11.3 us
    pallas_call x1, Pallas kernels, trailing_update(): pl.pallas_call(functools.partial(update_kernel, band=band), out_shape=jax...  10.4 us
    ppermute x6, waiting for transfers between devices, body(): lax.ppermute(own, axis, [(i, (i + hop) % size) for i in range(size)])  9.8 us
    ppermute x1, starting transfers between devices, body(): other = lax.ppermute(own, 'c', [(0, 1), (1, 0)])  8.72 us
  transfers between devices with their start and end apart: 9, of which 4 were waited for; matrix products, arithmetic and copies ran while one was open for 2% of the time, Pallas kernels for 27%

profile of v2, /device:TPU:1, one launch (start us, length us, event | category | flops | bytes accessed | tf_op | source)
XLA Modules:
  0.0 151.6 jit_solution(1823103631447737589)
XLA Ops:
  6.5 0.0 slice-start
  6.5 0.0 all-gather.3.cloned.1.call-start
  6.5 1.2 fusion.9
  7.7 0.1 copy.13
  7.8 0.1 copy.14
  7.9 0.7 fusion
  8.6 0.0 all-gather.3.cloned.1.call-update
  8.6 0.0 slice-done
  8.6 1.8 %broadcast_in_dim.3 = f32[32,24,800]{2,1,0:T(8,128)} broadcast(f32[24,800]{1,0:T(8,128)S(1)} %slice-done), dimensions={1,2} | broadcast | bytes 2534400 | tf_op jit(solution)/shard_map/broadcast_in_dim | solution.py:264
  10.4 11.3 %all-to-all-start = ((f32[32,24,800]{2,1,0:T(8,128)}), f32[32,24,800]{2,1,0:T(8,128)}, u32[]{:S(2)}, u32[]{:S(2)}) async-start(f32[32,24,800]{2,1,0:T(8,128)} %broadcast_in_dim.3), calls=%async_computation | async-start | bytes 5505024 | tf_op jit(solution)/shard_map/row_panel/all_to_all | solution.py:266
  21.7 0.1 copy.11
  21.7 30.0 %all-gather = f32[384,48]{1,0:T(8,128)S(1)} all-gather(f32[24,48]{1,0:T(8,128)S(1)} %copy.11), channel_id=2, replica_groups=mesh['x'=4,'y'=4,'c'=2,'z'=16] {'z'}, dimensions={0}, use_global_device_ids=true | all-gather | bytes 78336 | tf_op jit(solution)/shard_map/pivot_z/all_gather | solution.py:250
  51.8 0.1 reshape.146
  51.9 4.5 %collective-permute-start.2 = (f32[1,24,768]{2,1,0:T(8,128)S(1)}, f32[1,24,768]{2,1,0:T(8,128)S(1)}, u32[]{:S(2)}, u32[]{:S(2)}) collective-permute-start(f32[1,24,768]{2,1,0:T(8,128)S(1)} %reshape.146), channel_id=1, source_target_pairs={{0,96},{32,0},{64,32},{96,64},{1,97},{33,1},{65,33},{97,65},{2,98}... | collective-permute-start | bytes 221192 | tf_op jit(solution)/shard_map/pivot_y/ppermute | solution.py:256
  56.4 2.5 %collective-permute-start.1 = (f32[1,24,768]{2,1,0:T(8,128)S(1)}, f32[1,24,768]{2,1,0:T(8,128)S(1)}, u32[]{:S(2)}, u32[]{:S(2)}) collective-permute-start(f32[1,24,768]{2,1,0:T(8,128)S(1)} %reshape.146), channel_id=1, source_target_pairs={{0,64},{32,96},{64,0},{96,32},{1,65},{33,97},{65,1},{97,33},{2,66}... | collective-permute-start | bytes 221192 | tf_op jit(solution)/shard_map/pivot_y/ppermute | solution.py:256
  58.8 2.5 %collective-permute-start = (f32[1,24,768]{2,1,0:T(8,128)S(1)}, f32[1,24,768]{2,1,0:T(8,128)S(1)}, u32[]{:S(2)}, u32[]{:S(2)}) collective-permute-start(f32[1,24,768]{2,1,0:T(8,128)S(1)} %reshape.146), channel_id=1, source_target_pairs={{0,32},{32,64},{64,96},{96,0},{1,33},{33,65},{65,97},{97,1},{2,34}... | collective-permute-start | bytes 221192 | tf_op jit(solution)/shard_map/pivot_y/ppermute | solution.py:256
  61.3 4.2 %collective-permute-done = f32[1,24,768]{2,1,0:T(8,128)S(1)} collective-permute-done((f32[1,24,768]{2,1,0:T(8,128)S(1)}, f32[1,24,768]{2,1,0:T(8,128)S(1)}, u32[]{:S(2)}, u32[]{:S(2)}) %collective-permute-start) | collective-permute-done | bytes 73760 | tf_op jit(solution)/shard_map/pivot_y/ppermute | solution.py:256
  65.6 0.0 collective-permute-done.1
  65.6 0.0 collective-permute-done.2
  65.6 2.4 %collective-permute-start.3 = (f32[4,24,768]{2,1,0:T(8,128)S(1)}, f32[4,24,768]{2,1,0:T(8,128)S(1)}, u32[]{:S(2)}, u32[]{:S(2)}) collective-permute-start(f32[4,24,768]{2,1,0:T(8,128)S(1)} %get-tuple-element.7), channel_id=1, source_target_pairs={{0,128},{128,256},{256,384},{384,0},{1,129},{129,257},{257,385},{3... | collective-permute-start | bytes 884744 | tf_op jit(solution)/shard_map/pivot_x/ppermute | solution.py:256
  68.1 4.9 %collective-permute-start.4 = (f32[4,24,768]{2,1,0:T(8,128)S(1)}, f32[4,24,768]{2,1,0:T(8,128)S(1)}, u32[]{:S(2)}, u32[]{:S(2)}) collective-permute-start(f32[4,24,768]{2,1,0:T(8,128)S(1)} %get-tuple-element.7), channel_id=1, source_target_pairs={{0,256},{128,384},{256,0},{384,128},{1,257},{129,385},{257,1},{385... | collective-permute-start | bytes 884744 | tf_op jit(solution)/shard_map/pivot_x/ppermute | solution.py:256
  73.0 2.5 %collective-permute-start.5 = (f32[4,24,768]{2,1,0:T(8,128)S(1)}, f32[4,24,768]{2,1,0:T(8,128)S(1)}, u32[]{:S(2)}, u32[]{:S(2)}) collective-permute-start(f32[4,24,768]{2,1,0:T(8,128)S(1)} %get-tuple-element.7), channel_id=1, source_target_pairs={{0,384},{128,0},{256,128},{384,256},{1,385},{129,1},{257,129},{385... | collective-permute-start | bytes 884744 | tf_op jit(solution)/shard_map/pivot_x/ppermute | solution.py:256
  75.5 0.0 collective-permute-done.3
  75.6 2.9 %collective-permute-done.4 = f32[4,24,768]{2,1,0:T(8,128)S(1)} collective-permute-done((f32[4,24,768]{2,1,0:T(8,128)S(1)}, f32[4,24,768]{2,1,0:T(8,128)S(1)}, u32[]{:S(2)}, u32[]{:S(2)}) %collective-permute-start.4) | collective-permute-done | bytes 294944 | tf_op jit(solution)/shard_map/pivot_x/ppermute | solution.py:256
  78.5 2.7 %collective-permute-done.5 = f32[4,24,768]{2,1,0:T(8,128)S(1)} collective-permute-done((f32[4,24,768]{2,1,0:T(8,128)S(1)}, f32[4,24,768]{2,1,0:T(8,128)S(1)}, u32[]{:S(2)}, u32[]{:S(2)}) %collective-permute-start.5) | collective-permute-done | bytes 294944 | tf_op jit(solution)/shard_map/pivot_x/ppermute | solution.py:256
  81.2 8.7 %collective-permute-start.6 = (f32[16,24,768]{2,1,0:T(8,128)S(1)}, f32[16,24,768]{2,1,0:T(8,128)S(1)}, u32[]{:S(2)}, u32[]{:S(2)}) collective-permute-start(f32[16,24,768]{2,1,0:T(8,128)S(1)} %constant_dynamic-update-slice_fusion.4.own_ref), channel_id=1, source_target_pairs={{0,16},{16,0},{1,17},{17,1},{2,18},{18,2},{3,19},{19,3},{4,20},{20... | collective-permute-start | bytes 3538952 | tf_op jit(solution)/shard_map/pivot_core/ppermute | solution.py:261
  89.9 0.6 pad_add_fusion.1.place_ref
  90.6 1.8 %collective-permute-done.6.other_ref = f32[16,24,768]{2,1,0:T(8,128)S(1)} collective-permute-done((f32[16,24,768]{2,1,0:T(8,128)S(1)}, f32[16,24,768]{2,1,0:T(8,128)S(1)}, u32[]{:S(2)}, u32[]{:S(2)}) %collective-permute-start.6) | collective-permute-done | bytes 1179680 | tf_op jit(solution)/shard_map/pivot_core/ppermute | solution.py:261
  92.4 40.5 %pivot_inverse.1.inverse_hbm = f32[768,768]{1,0:T(8,128)S(1)} custom-call(s32[2,16]{1,0:T(2,128)S(1)} %pad_add_fusion.slot_ref, f32[16,24,768]{2,1,0:T(8,128)S(1)} %constant_dynamic-update-slice_fusion.4.own_ref, f32[16,24,768]{2,1,0:T(8,128)S(1)} %collective-permute-done.6.other_ref), custom_call_target="tpu_custom_call" | custom-call | flops 1 | bytes 8 | tf_op jit(solution)/shard_map/pivot_inverse/pallas_call | solution.py:141
  132.9 0.0 copy-start
  132.9 1.4 copy-done
  134.3 0.0 all-gather.3.cloned.1.call-done.column_hbm
  134.3 0.0 all-to-all-done
  134.3 10.4 %trailing_update.1 = f32[400,800]{1,0:T(8,128)} custom-call(s32[2]{0:T(128)} %pad_add_fusion.1.place_ref, f32[768,400]{1,0:T(8,128)} %all-gather.3.cloned.1.call-done.column_hbm, f32[768,768]{1,0:T(8,128)} %copy-done, f32[768,800]{1,0:T(8,128)} %bitcast.5.row_hbm, f32[400,800]{1,0:T(8,128)} %current_hbm.1), custom_call_target="tpu_custom_call" | custom-call | flops 963379200 | bytes 2560000 | tf_op jit(solution)/shard_map/trailing_update/pallas_call | solution.py:216
  (11 shorter events, 0.2 us)
Async XLA Ops:
  6.5 2.1 %slice-start = ((f32[400,800]{1,0:T(8,128)}), f32[24,800]{1,0:T(8,128)S(1)}, s32[]{:S(2)}) async-start(f32[400,800]{1,0:T(8,128)} %current_hbm.1), calls=%async_computation.2 | async-start | bytes 172032 | tf_op jit(solution)/shard_map/slice | solution.py:248
  6.5 127.8 %all-gather.3.cloned.1.call-start = ((), (), s32[]{:S(2)}) async-start(), calls=%async_computation.1 | async-start | bytes 1671168 | tf_op jit(solution)/shard_map/column_panel/all_gather | solution.py:263
  10.4 123.9 %all-to-all-start = ((f32[32,24,800]{2,1,0:T(8,128)}), f32[32,24,800]{2,1,0:T(8,128)}, u32[]{:S(2)}, u32[]{:S(2)}) async-start(f32[32,24,800]{2,1,0:T(8,128)} %broadcast_in_dim.3), calls=%async_computation | async-start | bytes 5505024 | tf_op jit(solution)/shard_map/row_panel/all_to_all | solution.py:266
  51.9 13.7 %collective-permute-start.2 = (f32[1,24,768]{2,1,0:T(8,128)S(1)}, f32[1,24,768]{2,1,0:T(8,128)S(1)}, u32[]{:S(2)}, u32[]{:S(2)}) collective-permute-start(f32[1,24,768]{2,1,0:T(8,128)S(1)} %reshape.146), channel_id=1, source_target_pairs={{0,96},{32,0},{64,32},{96,64},{1,97},{33,1},{65,33},{97,65},{2,98}... | collective-permute-start | bytes 221192 | tf_op jit(solution)/shard_map/pivot_y/ppermute | solution.py:256
  56.4 9.2 %collective-permute-start.1 = (f32[1,24,768]{2,1,0:T(8,128)S(1)}, f32[1,24,768]{2,1,0:T(8,128)S(1)}, u32[]{:S(2)}, u32[]{:S(2)}) collective-permute-start(f32[1,24,768]{2,1,0:T(8,128)S(1)} %reshape.146), channel_id=1, source_target_pairs={{0,64},{32,96},{64,0},{96,32},{1,65},{33,97},{65,1},{97,33},{2,66}... | collective-permute-start | bytes 221192 | tf_op jit(solution)/shard_map/pivot_y/ppermute | solution.py:256
  58.8 6.7 %collective-permute-start = (f32[1,24,768]{2,1,0:T(8,128)S(1)}, f32[1,24,768]{2,1,0:T(8,128)S(1)}, u32[]{:S(2)}, u32[]{:S(2)}) collective-permute-start(f32[1,24,768]{2,1,0:T(8,128)S(1)} %reshape.146), channel_id=1, source_target_pairs={{0,32},{32,64},{64,96},{96,0},{1,33},{33,65},{65,97},{97,1},{2,34}... | collective-permute-start | bytes 221192 | tf_op jit(solution)/shard_map/pivot_y/ppermute | solution.py:256
  65.6 9.9 %collective-permute-start.3 = (f32[4,24,768]{2,1,0:T(8,128)S(1)}, f32[4,24,768]{2,1,0:T(8,128)S(1)}, u32[]{:S(2)}, u32[]{:S(2)}) collective-permute-start(f32[4,24,768]{2,1,0:T(8,128)S(1)} %get-tuple-element.7), channel_id=1, source_target_pairs={{0,128},{128,256},{256,384},{384,0},{1,129},{129,257},{257,385},{3... | collective-permute-start | bytes 884744 | tf_op jit(solution)/shard_map/pivot_x/ppermute | solution.py:256
  68.1 10.4 %collective-permute-start.4 = (f32[4,24,768]{2,1,0:T(8,128)S(1)}, f32[4,24,768]{2,1,0:T(8,128)S(1)}, u32[]{:S(2)}, u32[]{:S(2)}) collective-permute-start(f32[4,24,768]{2,1,0:T(8,128)S(1)} %get-tuple-element.7), channel_id=1, source_target_pairs={{0,256},{128,384},{256,0},{384,128},{1,257},{129,385},{257,1},{385... | collective-permute-start | bytes 884744 | tf_op jit(solution)/shard_map/pivot_x/ppermute | solution.py:256
  73.0 8.2 %collective-permute-start.5 = (f32[4,24,768]{2,1,0:T(8,128)S(1)}, f32[4,24,768]{2,1,0:T(8,128)S(1)}, u32[]{:S(2)}, u32[]{:S(2)}) collective-permute-start(f32[4,24,768]{2,1,0:T(8,128)S(1)} %get-tuple-element.7), channel_id=1, source_target_pairs={{0,384},{128,0},{256,128},{384,256},{1,385},{129,1},{257,129},{385... | collective-permute-start | bytes 884744 | tf_op jit(solution)/shard_map/pivot_x/ppermute | solution.py:256
  81.2 11.2 %collective-permute-start.6 = (f32[16,24,768]{2,1,0:T(8,128)S(1)}, f32[16,24,768]{2,1,0:T(8,128)S(1)}, u32[]{:S(2)}, u32[]{:S(2)}) collective-permute-start(f32[16,24,768]{2,1,0:T(8,128)S(1)} %constant_dynamic-update-slice_fusion.4.own_ref), channel_id=1, source_target_pairs={{0,16},{16,0},{1,17},{17,1},{2,18},{18,2},{3,19},{19,3},{4,20},{20... | collective-permute-start | bytes 3538952 | tf_op jit(solution)/shard_map/pivot_core/ppermute | solution.py:261
  132.9 1.4 copy-start
Sparse Core Ops, SparseCore 0:
  9.4 69.0 all-gather.2

commit v3 on v2

--- a/solution.py
+++ b/solution.py
@@ -94,17 +94,15 @@
     return jnp.dot(left, right, preferred_element_type=F32)
 
 
-def inverse_kernel(slot_ref, own_ref, other_ref, out_ref, left_ref, right_ref, diagonal_ref):
-    pairs, band, order = own_ref.shape
+def eliminate(first, last, out_ref, left_ref, right_ref, diagonal_ref):
+    order = out_ref.shape[0]
     blocks = order // TILE
-    for i in range(pairs):
-        out_ref[pl.ds(pl.multiple_of(slot_ref[0, i] * band, 8), band), :] = own_ref[i]
-        out_ref[pl.ds(pl.multiple_of(slot_ref[1, i] * band, 8), band), :] = other_ref[i]
     unit = lax.broadcasted_iota(jnp.int32, (TILE, TILE), 0) == lax.broadcasted_iota(
         jnp.int32, (TILE, TILE), 1
     )
     unit = jnp.where(unit, 1.0, 0.0)
-    diagonal_ref[...] = out_ref[0:TILE, 0:TILE]
+    start = slice(TILE * first, TILE * first + TILE)
+    diagonal_ref[...] = out_ref[start, start]
     left_ref[...] = jnp.zeros(left_ref.shape, BF16)
     right_ref[...] = jnp.zeros(right_ref.shape, BF16)
 
@@ -131,17 +129,30 @@
         diagonal_ref[...] = out_ref[after, after] - product(left_ref[after, :], right_ref[:, after])
         return carry
 
-    lax.fori_loop(0, blocks, step, 0)
+    lax.fori_loop(first, last, step, 0)
     apply_last()
 
 
-def pivot_inverse(slots, own, other):
-    order = own.shape[2]
+def first_kernel(slot_ref, own_ref, other_ref, out_ref, *scratch, last):
+    pairs, band, _ = own_ref.shape
+    for i in range(pairs):
+        out_ref[pl.ds(pl.multiple_of(slot_ref[0, i] * band, 8), band), :] = own_ref[i]
+        out_ref[pl.ds(pl.multiple_of(slot_ref[1, i] * band, 8), band), :] = other_ref[i]
+    eliminate(0, last, out_ref, *scratch)
+
+
+def second_kernel(part_ref, out_ref, *scratch, first):
+    out_ref[...] = part_ref[...]
+    eliminate(first, out_ref.shape[0] // TILE, out_ref, *scratch)
+
+
+def pivot_sweep(kernel, order, flops, name, *arrays):
     vmem = pl.BlockSpec(memory_space=pltpu.VMEM)
+    small = pl.BlockSpec(memory_space=pltpu.SMEM)
     return pl.pallas_call(
-        inverse_kernel,
+        kernel,
         out_shape=jax.ShapeDtypeStruct((order, order), F32),
-        in_specs=[pl.BlockSpec(memory_space=pltpu.SMEM), vmem, vmem],
+        in_specs=[small if array.dtype == jnp.int32 else vmem for array in arrays],
         out_specs=vmem,
         scratch_shapes=[
             pltpu.VMEM((order, 6 * TILE), BF16),
@@ -149,9 +160,9 @@
             pltpu.VMEM((TILE, TILE), F32),
         ],
         compiler_params=pltpu.CompilerParams(vmem_limit_bytes=20 * 1024 * 1024),
-        cost_estimate=pl.CostEstimate(flops=1, bytes_accessed=8, transcendentals=0),
-        name="pivot_inverse",
-    )(slots, own, other)
+        cost_estimate=pl.CostEstimate(flops=flops, bytes_accessed=8, transcendentals=0),
+        name=name,
+    )(*arrays)
 
 
 def update_kernel(
@@ -247,29 +258,31 @@
     )
     rowband = matrix[0:band, :]
     with jax.named_scope("pivot_z"):
-        pivot = lax.all_gather(strip[0:band, :], "z", axis=0, tiled=False)
-    own = pivot.transpose(1, 0, 2).reshape(1, band, K * B)
-    for axis in ("y", "x"):
-        size = lax.axis_size(axis)
-        with jax.named_scope("pivot_" + axis):
-            pieces = [own] + [
-                lax.ppermute(own, axis, [(i, (i + hop) % size) for i in range(size)])
-                for hop in range(1, size)
-            ]
-        own = jnp.concatenate(pieces, axis=0)
+        pivot = lax.all_to_all(
+            jnp.broadcast_to(strip[0:band, :], (depth, band, groups * band)), "z", 0, 0
+        )
+    pivot = pivot.transpose(1, 0, 2).reshape(band, K * B)
+    with jax.named_scope("pivot_xy"):
+        own = lax.all_to_all(jnp.broadcast_to(pivot, (chips, band, K * B)), ("x", "y"), 0, 0)
     with jax.named_scope("pivot_core"):
         other = lax.ppermute(own, "c", [(0, 1), (1, 0)])
     with jax.named_scope("column_panel"):
         column = lax.all_gather(strip.T, "z", axis=0, tiled=True)
     spread = jnp.broadcast_to(rowband, (2 * chips, band, cols))
+    spread, other = lax.optimization_barrier((spread, other))
     with jax.named_scope("row_panel"):
         row = lax.all_to_all(spread, ("x", "y", "c"), 0, 0)
-    hops = jnp.arange(chips, dtype=jnp.int32)
-    size_x, size_y = lax.axis_size("x"), lax.axis_size("y")
-    from_x = (lax.axis_index("x") - hops // size_y) % size_x
-    from_y = (lax.axis_index("y") - hops % size_y) % size_y
-    first = 2 * (from_x * size_y + from_y)
-    inverse = pivot_inverse(jnp.stack([first + core, first + 1 - core]), own, other)
+    first = 2 * jnp.arange(chips, dtype=jnp.int32)
+    slots = jnp.stack([first + core, first + 1 - core])
+    order = K * B
+    half = 2
+    part = pivot_sweep(
+        functools.partial(first_kernel, last=half), order, 1, "sweep_first", slots, own, other
+    )
+    column, part = lax.optimization_barrier((column, part))
+    inverse = pivot_sweep(
+        functools.partial(second_kernel, first=half), order, 10**12, "sweep_second", part
+    )
     return trailing_update(
         place, matrix, column, row.reshape(K * B, cols), inverse, band
     )

time: 152 us -> 162 us (1.066)
  waiting for transfers between devices: 11.6 us -> 24.3 us
  blocking collectives: 30 us -> 22.2 us
  local copies, waits for them, and re-layouts: 4.87 us -> 8.6 us
  Pallas kernels: 51 us -> 53 us
    all_gather x1 -> x0, blocking collectives: 30 us -> none  [body(): pivot = lax.all_gather(strip[0:band, :], 'z', axis=0, tiled=False)]
    all_to_all x0 -> x1, blocking collectives: none -> 22.2 us  [body(): lax.all_to_all(jnp.broadcast_to(pivot, (chips, band, K * B)), ('x', 'y'),...]
    ppermute x6 -> x0, starting transfers between devices: 19.3 us -> none  [body(): lax.ppermute(own, axis, [(i, (i + hop) % size) for i in range(size)])]
    all_to_all x0 -> x1, starting transfers between devices: none -> 15.7 us  [body(): lax.all_to_all(jnp.broadcast_to(strip[0:band, :], (depth, band, groups *...]
    all_to_all x0 -> x1, waiting for transfers between devices: none -> 11 us  [body(): lax.all_to_all(jnp.broadcast_to(strip[0:band, :], (depth, band, groups *...]
    ppermute x6 -> x0, waiting for transfers between devices: 9.8 us -> none  [body(): lax.ppermute(own, axis, [(i, (i + hop) % size) for i in range(size)])]
    all_to_all x1, waiting for transfers between devices: 0.01 us -> 6.65 us  [body(): row = lax.all_to_all(spread, ('x', 'y', 'c'), 0, 0)]
    all_to_all x1, starting transfers between devices: 11.3 us -> 16.4 us  [body(): row = lax.all_to_all(spread, ('x', 'y', 'c'), 0, 0)]
  transfers between devices with their start and end apart: 9 -> 4, of which waited for: 4 -> 4; matrix products, arithmetic and copies ran while one was open for 2% -> 3% of each run, Pallas kernels for 27% -> 26%
where the time goes in v3:
time: 162 us
  Pallas kernels  53 us (33%)
  starting transfers between devices  37.9 us (23%)
  waiting for transfers between devices  24.3 us (15%)
  blocking collectives  22.2 us (14%)
  between operations  13.5 us (8%)
  local copies, waits for them, and re-layouts  8.6 us (5%)
  other arithmetic  2.09 us (1%)
    pallas_call x2, Pallas kernels, pivot_sweep(): pl.pallas_call(kernel, out_shape=jax.ShapeDtypeStruct((order, order), F32...  42.5 us
    all_to_all x1, blocking collectives, body(): lax.all_to_all(jnp.broadcast_to(pivot, (chips, band, K * B)), ('x', 'y'),...  22.2 us
    all_to_all x1, starting transfers between devices, body(): row = lax.all_to_all(spread, ('x', 'y', 'c'), 0, 0)  16.4 us
    all_to_all x1, starting transfers between devices, body(): lax.all_to_all(jnp.broadcast_to(strip[0:band, :], (depth, band, groups *...  15.7 us
    all_to_all x1, waiting for transfers between devices, body(): lax.all_to_all(jnp.broadcast_to(strip[0:band, :], (depth, band, groups *...  11 us
    pallas_call x1, Pallas kernels, trailing_update(): pl.pallas_call(functools.partial(update_kernel, band=band), out_shape=jax...  10.4 us
    all_to_all x1, waiting for transfers between devices, body(): row = lax.all_to_all(spread, ('x', 'y', 'c'), 0, 0)  6.65 us
    ppermute x1, starting transfers between devices, body(): other = lax.ppermute(own, 'c', [(0, 1), (1, 0)])  5.7 us
  transfers between devices with their start and end apart: 4, of which 4 were waited for; matrix products, arithmetic and copies ran while one was open for 3% of the time, Pallas kernels for 26%

profile of v3, /device:TPU:1, one launch (start us, length us, event | category | flops | bytes accessed | tf_op | source)
XLA Modules:
  0.0 161.6 jit_solution(1121204917235168986)
XLA Ops:
  6.5 1.1 fusion.3
  7.7 0.1 copy.12
  7.8 0.1 copy.13
  7.9 0.1 copy.10
  8.0 0.8 reshape.25
  8.8 15.7 %all-to-all-start = ((f32[16,1,1152]{2,1,0:T(1,128)}), f32[16,1,1152]{2,1,0:T(1,128)S(1)}, u32[]{:S(2)}, u32[]{:S(2)}) async-start(f32[16,1,1152]{2,1,0:T(1,128)} %reshape.25), calls=%async_computation | async-start | bytes 147456 | tf_op jit(solution)/shard_map/pivot_z/all_to_all | solution.py:261
  24.6 0.0 all-gather.2.cloned.1.call-start
  24.6 0.6 fusion
  25.3 0.0 all-gather.2.cloned.1.call-update
  25.3 11.0 %all-to-all-done = f32[16,1,1152]{2,1,0:T(1,128)S(1)} async-done(((f32[16,1,1152]{2,1,0:T(1,128)}), f32[16,1,1152]{2,1,0:T(1,128)S(1)}, u32[]{:S(2)}, u32[]{:S(2)}) %all-to-all-start) | async-done | bytes 73760 | tf_op jit(solution)/shard_map/pivot_z/all_to_all | solution.py:261
  36.3 0.5 broadcast.43
  36.8 0.8 reduce
  37.6 0.1 reshape.26
  37.8 0.1 reshape.23
  37.9 0.1 broadcast_in_dim.10
  38.0 0.0 slice-start
  38.0 22.2 %all_to_all.15.own_ref = f32[16,24,768]{2,1,0:T(8,128)S(1)} all-to-all(f32[16,24,768]{2,1,0:T(8,128)S(1)} %broadcast_in_dim.10), channel_id=1, replica_groups=mesh['x'=4,'y'=4,'c'=2,'z'=16] {'x','y'}, dimensions={0} | all-to-all | bytes 2359296 | tf_op jit(solution)/shard_map/pivot_xy/all_to_all | solution.py:266
  60.2 5.7 %collective-permute-start = (f32[16,24,768]{2,1,0:T(8,128)S(1)}, f32[16,24,768]{2,1,0:T(8,128)S(1)}, u32[]{:S(2)}, u32[]{:S(2)}) collective-permute-start(f32[16,24,768]{2,1,0:T(8,128)S(1)} %all_to_all.15.own_ref), channel_id=1, source_target_pairs={{0,16},{16,0},{1,17},{17,1},{2,18},{18,2},{3,19},{19,3},{4,20},{20... | collective-permute-start | bytes 3538952 | tf_op jit(solution)/shard_map/pivot_core/ppermute | solution.py:268
  65.9 0.6 pad_add_fusion.1.place_ref
  66.6 1.8 %collective-permute-done.other_ref = f32[16,24,768]{2,1,0:T(8,128)S(1)} collective-permute-done((f32[16,24,768]{2,1,0:T(8,128)S(1)}, f32[16,24,768]{2,1,0:T(8,128)S(1)}, u32[]{:S(2)}, u32[]{:S(2)}) %collective-permute-start) | collective-permute-done | bytes 1179680 | tf_op jit(solution)/shard_map/pivot_core/ppermute | solution.py:268
  68.4 0.0 copy-start.1
  68.4 1.0 copy-done.1
  69.4 0.0 slice-done
  69.4 1.8 %broadcast_in_dim.11 = f32[32,24,800]{2,1,0:T(8,128)} broadcast(f32[24,800]{1,0:T(8,128)S(1)} %slice-done), dimensions={1,2} | broadcast | bytes 2534400 | tf_op jit(solution)/shard_map/broadcast_in_dim | solution.py:271
  71.2 0.0 copy-start.2
  71.2 1.3 copy-done.2
  72.4 15.2 %sweep_first.1.part_ref = f32[768,768]{1,0:T(8,128)S(1)} custom-call(s32[2,16]{1,0:T(2,128)S(1)} %pad_add_fusion.slot_ref, f32[16,24,768]{2,1,0:T(8,128)S(1)} %all_to_all.15.own_ref, f32[16,24,768]{2,1,0:T(8,128)S(1)} %copy-done.2), custom_call_target="tpu_custom_call" | custom-call | flops 1 | bytes 8 | tf_op jit(solution)/shard_map/sweep_first/pallas_call | solution.py:152
  87.7 4.8 %all-gather.2.cloned.1.call-done.column_hbm = f32[768,400]{1,0:T(8,128)} async-done(((f32[48,400]{1,0:T(8,128)}), f32[768,400]{1,0:T(8,128)}) %all-gather.2.cloned.1.call-update) | async-done | bytes 1228816 | tf_op jit(solution)/shard_map/column_panel/all_gather | solution.py:270
  92.5 16.4 %all-to-all-start.2 = ((f32[32,24,800]{2,1,0:T(8,128)}), f32[32,24,800]{2,1,0:T(8,128)}, u32[]{:S(2)}, u32[]{:S(2)}) async-start(f32[32,24,800]{2,1,0:T(8,128)} %broadcast_in_dim.11), calls=%async_computation.2 | async-start | bytes 5505024 | tf_op jit(solution)/shard_map/row_panel/all_to_all | solution.py:274
  108.9 27.3 %sweep_second.1.inverse_hbm = f32[768,768]{1,0:T(8,128)S(1)} custom-call(f32[768,768]{1,0:T(8,128)S(1)} %sweep_first.1.part_ref), custom_call_target="tpu_custom_call" | custom-call | flops 999999995904 | bytes 8 | tf_op jit(solution)/shard_map/sweep_second/pallas_call | solution.py:152
  136.2 0.0 copy-start
  136.2 1.4 copy-done
  137.6 6.7 %all-to-all-done.2 = f32[32,24,800]{2,1,0:T(8,128)} async-done(((f32[32,24,800]{2,1,0:T(8,128)}), f32[32,24,800]{2,1,0:T(8,128)}, u32[]{:S(2)}, u32[]{:S(2)}) %all-to-all-start.2) | async-done | bytes 2457632 | tf_op jit(solution)/shard_map/row_panel/all_to_all | solution.py:274
  144.3 10.4 %trailing_update.1 = f32[400,800]{1,0:T(8,128)} custom-call(s32[2]{0:T(128)} %pad_add_fusion.1.place_ref, f32[768,400]{1,0:T(8,128)} %all-gather.2.cloned.1.call-done.column_hbm, f32[768,768]{1,0:T(8,128)} %copy-done, f32[768,800]{1,0:T(8,128)} %bitcast.4.row_hbm, f32[400,800]{1,0:T(8,128)} %current_hbm.1), custom_call_target="tpu_custom_call" | custom-call | flops 963379200 | bytes 2560000 | tf_op jit(solution)/shard_map/trailing_update/pallas_call | solution.py:227
  (5 shorter events, 0.1 us)
Async XLA Ops:
  8.8 27.5 %all-to-all-start = ((f32[16,1,1152]{2,1,0:T(1,128)}), f32[16,1,1152]{2,1,0:T(1,128)S(1)}, u32[]{:S(2)}, u32[]{:S(2)}) async-start(f32[16,1,1152]{2,1,0:T(1,128)} %reshape.25), calls=%async_computation | async-start | bytes 147456 | tf_op jit(solution)/shard_map/pivot_z/all_to_all | solution.py:261
  24.6 67.9 %all-gather.2.cloned.1.call-start = ((), (), s32[]{:S(2)}) async-start(), calls=%async_computation.3 | async-start | bytes 1671168 | tf_op jit(solution)/shard_map/column_panel/all_gather | solution.py:270
  38.0 31.4 %slice-start = ((f32[400,800]{1,0:T(8,128)}), f32[24,800]{1,0:T(8,128)S(1)}, s32[]{:S(2)}) async-start(f32[400,800]{1,0:T(8,128)} %current_hbm.1), calls=%async_computation.4 | async-start | bytes 172032 | tf_op jit(solution)/shard_map/slice | solution.py:259
  60.2 8.2 %collective-permute-start = (f32[16,24,768]{2,1,0:T(8,128)S(1)}, f32[16,24,768]{2,1,0:T(8,128)S(1)}, u32[]{:S(2)}, u32[]{:S(2)}) collective-permute-start(f32[16,24,768]{2,1,0:T(8,128)S(1)} %all_to_all.15.own_ref), channel_id=1, source_target_pairs={{0,16},{16,0},{1,17},{17,1},{2,18},{18,2},{3,19},{19,3},{4,20},{20... | collective-permute-start | bytes 3538952 | tf_op jit(solution)/shard_map/pivot_core/ppermute | solution.py:268
  68.4 1.0 copy-start.1
  71.2 1.3 copy-start.2
  92.5 51.7 %all-to-all-start.2 = ((f32[32,24,800]{2,1,0:T(8,128)}), f32[32,24,800]{2,1,0:T(8,128)}, u32[]{:S(2)}, u32[]{:S(2)}) async-start(f32[32,24,800]{2,1,0:T(8,128)} %broadcast_in_dim.11), calls=%async_computation.2 | async-start | bytes 5505024 | tf_op jit(solution)/shard_map/row_panel/all_to_all | solution.py:274
  136.2 1.4 copy-start
Sparse Core Ops, SparseCore 0:
  27.5 64.9 all-gather.1

commit v4 on v3

--- a/solution.py
+++ b/solution.py
@@ -94,7 +94,7 @@
     return jnp.dot(left, right, preferred_element_type=F32)
 
 
-def eliminate(first, last, out_ref, left_ref, right_ref, diagonal_ref):
+def eliminate(first, last, done, out_ref, left_ref, right_ref, diagonal_ref):
     order = out_ref.shape[0]
     blocks = order // TILE
     unit = lax.broadcasted_iota(jnp.int32, (TILE, TILE), 0) == lax.broadcasted_iota(
@@ -106,10 +106,12 @@
     left_ref[...] = jnp.zeros(left_ref.shape, BF16)
     right_ref[...] = jnp.zeros(right_ref.shape, BF16)
 
-    def apply_last():
+    def apply_last(done=None):
         for c in range(blocks):
             here = slice(TILE * c, TILE * c + TILE)
             out_ref[:, here] = out_ref[:, here] - product(left_ref[...], right_ref[:, here])
+            if done is not None:
+                done(here)
 
     def step(k, carry):
         here = pl.ds(pl.multiple_of(k * TILE, TILE), TILE)
@@ -130,36 +132,43 @@
         return carry
 
     lax.fori_loop(first, last, step, 0)
-    apply_last()
-
-
-def first_kernel(slot_ref, own_ref, other_ref, out_ref, *scratch, last):
-    pairs, band, _ = own_ref.shape
-    for i in range(pairs):
-        out_ref[pl.ds(pl.multiple_of(slot_ref[0, i] * band, 8), band), :] = own_ref[i]
-        out_ref[pl.ds(pl.multiple_of(slot_ref[1, i] * band, 8), band), :] = other_ref[i]
-    eliminate(0, last, out_ref, *scratch)
-
-
-def second_kernel(part_ref, out_ref, *scratch, first):
-    out_ref[...] = part_ref[...]
-    eliminate(first, out_ref.shape[0] // TILE, out_ref, *scratch)
-
-
-def pivot_sweep(kernel, order, flops, name, *arrays):
+    apply_last(done)
+
+
+def sweep_kernel(*refs, first, last, joined):
+    out_hbm, left_ref, right_ref, diagonal_ref, work_ref, sem = refs[-6:]
+    if joined:
+        work_ref[...] = refs[0][...]
+    else:
+        slot_ref, own_ref, other_ref = refs[:3]
+        pairs, band, _ = own_ref.shape
+        for i in range(pairs):
+            work_ref[pl.ds(pl.multiple_of(slot_ref[0, i] * band, 8), band), :] = own_ref[i]
+            work_ref[pl.ds(pl.multiple_of(slot_ref[1, i] * band, 8), band), :] = other_ref[i]
+
+    def store(here):
+        pltpu.make_async_copy(work_ref.at[:, here], out_hbm.at[:, here], sem).start()
+
+    eliminate(first, last, store, work_ref, left_ref, right_ref, diagonal_ref)
+    pltpu.make_async_copy(work_ref, out_hbm, sem).wait()
+
+
+def pivot_sweep(first, last, order, flops, name, *arrays):
     vmem = pl.BlockSpec(memory_space=pltpu.VMEM)
     small = pl.BlockSpec(memory_space=pltpu.SMEM)
     return pl.pallas_call(
-        kernel,
+        functools.partial(sweep_kernel, first=first, last=last, joined=len(arrays) == 1),
         out_shape=jax.ShapeDtypeStruct((order, order), F32),
         in_specs=[small if array.dtype == jnp.int32 else vmem for array in arrays],
-        out_specs=vmem,
+        out_specs=pl.BlockSpec(memory_space=pl.ANY),
         scratch_shapes=[
             pltpu.VMEM((order, 6 * TILE), BF16),
             pltpu.VMEM((6 * TILE, order), BF16),
             pltpu.VMEM((TILE, TILE), F32),
+            pltpu.VMEM((order, order), F32),
+            pltpu.SemaphoreType.DMA(()),
         ],
-        compiler_params=pltpu.CompilerParams(vmem_limit_bytes=20 * 1024 * 1024),
+        compiler_params=pltpu.CompilerParams(vmem_limit_bytes=54 * 1024 * 1024),
         cost_estimate=pl.CostEstimate(flops=flops, bytes_accessed=8, transcendentals=0),
         name=name,
     )(*arrays)
@@ -191,7 +200,7 @@
     pick = jnp.where(iota(shape, 0) == iota(shape, 1) + my_rows, -1.0, 0.0)
     column = jnp.where(iota(shape, 1) < band, pick, column_ref[...])
     loads[1].wait()
-    scaled = jnp.dot(inverse_ref[...], column, precision=HIGHEST, preferred_element_type=F32).T
+    scaled = product(left_parts(inverse_ref[...]), right_parts(column)).T
 
     def strip_of(shape):
         at = iota(shape, 1)
@@ -213,8 +222,9 @@
     inside, _ = strip_of(shape)
     scaled_high, scaled_low, _ = three_parts(scaled)
     row_high, row_low, _ = three_parts(row)
-    change = product(scaled_high, row_high) + (
-        product(scaled_high, row_low) + product(scaled_low, row_high)
+    change = product(
+        jnp.concatenate([scaled_high, scaled_high, scaled_low], axis=1),
+        jnp.concatenate([row_high, row_low, row_high], axis=0),
     )
     loads[3].wait()
     base = jnp.where(inside | (iota(shape, 0) < band), 0.0, current_ref[...])
@@ -258,10 +268,9 @@
     )
     rowband = matrix[0:band, :]
     with jax.named_scope("pivot_z"):
-        pivot = lax.all_to_all(
-            jnp.broadcast_to(strip[0:band, :], (depth, band, groups * band)), "z", 0, 0
-        )
-    pivot = pivot.transpose(1, 0, 2).reshape(band, K * B)
+        padded = jnp.pad(strip[0:band, :], ((0, 0), (0, TILE - groups * band)))
+        pivot = lax.all_to_all(jnp.broadcast_to(padded, (depth, band, TILE)), "z", 0, 0)
+    pivot = pivot[:, :, : groups * band].transpose(1, 0, 2).reshape(band, K * B)
     with jax.named_scope("pivot_xy"):
         own = lax.all_to_all(jnp.broadcast_to(pivot, (chips, band, K * B)), ("x", "y"), 0, 0)
     with jax.named_scope("pivot_core"):
@@ -275,14 +284,11 @@
     first = 2 * jnp.arange(chips, dtype=jnp.int32)
     slots = jnp.stack([first + core, first + 1 - core])
     order = K * B
-    half = 2
-    part = pivot_sweep(
-        functools.partial(first_kernel, last=half), order, 1, "sweep_first", slots, own, other
-    )
+    half = 4
+    blocks = order // TILE
+    part = pivot_sweep(0, half, order, 1, "sweep_first", slots, own, other)
     column, part = lax.optimization_barrier((column, part))
-    inverse = pivot_sweep(
-        functools.partial(second_kernel, first=half), order, 10**12, "sweep_second", part
-    )
+    inverse = pivot_sweep(half, blocks, order, 24 * 10**9, "sweep_second", part)
     return trailing_update(
         place, matrix, column, row.reshape(K * B, cols), inverse, band
     )

time: 162 us -> 154 us (0.951)
  the two profiles are of different devices: /device:TPU:1 before, /device:TPU:2 now
where the time goes in v4:
time: 154 us
  Pallas kernels  57.6 us (37%)
  blocking collectives  31.4 us (20%)
  waiting for transfers between devices  28 us (18%)
  starting transfers between devices  15.2 us (10%)
  between operations  13.5 us (9%)
  local copies, waits for them, and re-layouts  6.19 us (4%)
  other arithmetic  1.86 us (1%)
    pallas_call x2, Pallas kernels, pivot_sweep(): pl.pallas_call(functools.partial(sweep_kernel, first=first, last=last, jo...  47.3 us
    all_to_all x1, blocking collectives, body(): lax.all_to_all(jnp.broadcast_to(padded, (depth, band, TILE)), 'z', 0, 0)  31.4 us
    all_gather x1, waiting for transfers between devices, body(): column = lax.all_gather(strip.T, 'z', axis=0, tiled=True)  13.2 us
    all_to_all x1, waiting for transfers between devices, body(): lax.all_to_all(jnp.broadcast_to(pivot, (chips, band, K * B)), ('x', 'y'),...  11.9 us
    pallas_call x1, Pallas kernels, trailing_update(): pl.pallas_call(functools.partial(update_kernel, band=band), out_shape=jax...  10.3 us
    all_to_all x1, starting transfers between devices, body(): lax.all_to_all(jnp.broadcast_to(pivot, (chips, band, K * B)), ('x', 'y'),...  7.61 us
    all_to_all x1, starting transfers between devices, body(): row = lax.all_to_all(spread, ('x', 'y', 'c'), 0, 0)  5.64 us
  transfers between devices with their start and end apart: 4, of which 3 were waited for; matrix products, arithmetic and copies ran while one was open for 2% of the time, Pallas kernels for 31%

profile of v4, /device:TPU:2, one launch (start us, length us, event | category | flops | bytes accessed | tf_op | source)
XLA Modules:
  0.0 153.8 jit_solution(343242587691795517)
XLA Ops:
  6.5 1.1 fusion.3
  7.7 0.1 copy.12
  7.8 0.1 copy.13
  7.9 0.1 copy.14
  8.0 31.4 %all_to_all.15 = f32[16,24,128]{2,1,0:T(8,128)S(1)} all-to-all(f32[16,24,128]{2,1,0:T(8,128)S(1)} %broadcast_in_dim.9), channel_id=1, replica_groups=mesh['x'=4,'y'=4,'c'=2,'z'=16] {'z'}, dimensions={0} | all-to-all | bytes 393216 | tf_op jit(solution)/shard_map/pivot_z/all_to_all | solution.py:272
  39.5 0.1 reshape.23
  39.6 1.1 broadcast_in_dim.10
  40.7 0.0 slice-start
  40.7 7.6 %all-to-all-start.1 = ((f32[16,24,768]{2,1,0:T(8,128)}), f32[16,24,768]{2,1,0:T(8,128)S(1)}, u32[]{:S(2)}, u32[]{:S(2)}) async-start(f32[16,24,768]{2,1,0:T(8,128)} %broadcast_in_dim.10), calls=%async_computation.1 | async-start | bytes 2359296 | tf_op jit(solution)/shard_map/pivot_xy/all_to_all | solution.py:275
  48.3 0.0 all-gather.2.cloned.1.call-start
  48.4 0.6 fusion
  49.0 0.0 all-gather.2.cloned.1.call-update
  49.1 11.9 %all-to-all-done.1.refs_1_ = f32[16,24,768]{2,1,0:T(8,128)S(1)} async-done(((f32[16,24,768]{2,1,0:T(8,128)}), f32[16,24,768]{2,1,0:T(8,128)S(1)}, u32[]{:S(2)}, u32[]{:S(2)}) %all-to-all-start.1) | async-done | bytes 1179680 | tf_op jit(solution)/shard_map/pivot_xy/all_to_all | solution.py:275
  61.0 0.0 copy-start.1
  61.0 1.9 %collective-permute-start = (f32[16,24,768]{2,1,0:T(8,128)S(1)}, f32[16,24,768]{2,1,0:T(8,128)S(1)}, u32[]{:S(2)}, u32[]{:S(2)}) collective-permute-start(f32[16,24,768]{2,1,0:T(8,128)S(1)} %all-to-all-done.1.refs_1_), channel_id=1, source_target_pairs={{0,16},{16,0},{1,17},{17,1},{2,18},{18,2},{3,19},{19,3},{4,20},{20... | collective-permute-start | bytes 3538952 | tf_op jit(solution)/shard_map/pivot_core/ppermute | solution.py:277
  63.0 2.8 %collective-permute-done.refs_2_ = f32[16,24,768]{2,1,0:T(8,128)S(1)} collective-permute-done((f32[16,24,768]{2,1,0:T(8,128)S(1)}, f32[16,24,768]{2,1,0:T(8,128)S(1)}, u32[]{:S(2)}, u32[]{:S(2)}) %collective-permute-start) | collective-permute-done | bytes 1179680 | tf_op jit(solution)/shard_map/pivot_core/ppermute | solution.py:277
  65.8 0.0 slice-done
  65.8 0.0 copy-start.2
  65.8 1.8 %broadcast_in_dim.11 = f32[32,24,800]{2,1,0:T(8,128)} broadcast(f32[24,800]{1,0:T(8,128)S(1)} %slice-done), dimensions={1,2} | broadcast | bytes 2534400 | tf_op jit(solution)/shard_map/broadcast_in_dim | solution.py:280
  67.6 0.0 copy-done.1
  67.6 0.1 copy-done.2
  67.7 5.6 %all-to-all-start.2 = ((f32[32,24,800]{2,1,0:T(8,128)}), f32[32,24,800]{2,1,0:T(8,128)S(1)}, u32[]{:S(2)}, u32[]{:S(2)}) async-start(f32[32,24,800]{2,1,0:T(8,128)} %broadcast_in_dim.11), calls=%async_computation.2 | async-start | bytes 5505024 | tf_op jit(solution)/shard_map/row_panel/all_to_all | solution.py:283
  73.3 0.6 pad_add_fusion.1.place_ref
  74.0 0.6 pad_add_fusion.refs_0_
  74.5 29.7 %sweep_first.1.refs_0_ = f32[768,768]{1,0:T(8,128)} custom-call(s32[2,16]{1,0:T(2,128)} %pad_add_fusion.refs_0_, f32[16,24,768]{2,1,0:T(8,128)} %copy-done.1, f32[16,24,768]{2,1,0:T(8,128)} %copy-done.2), custom_call_target="tpu_custom_call" | custom-call | flops 1 | bytes 8 | tf_op jit(solution)/shard_map/sweep_first/pallas_call | solution.py:159
  104.2 13.2 %all-gather.2.cloned.1.call-done.column_hbm = f32[768,400]{1,0:T(8,128)} async-done(((f32[48,400]{1,0:T(8,128)}), f32[768,400]{1,0:T(8,128)}) %all-gather.2.cloned.1.call-update) | async-done | bytes 1228816 | tf_op jit(solution)/shard_map/column_panel/all_gather | solution.py:279
  117.5 17.5 %sweep_second.1.inverse_hbm = f32[768,768]{1,0:T(8,128)} custom-call(f32[768,768]{1,0:T(8,128)} %sweep_first.1.refs_0_), custom_call_target="tpu_custom_call" | custom-call | flops 24000000000 | bytes 8 | tf_op jit(solution)/shard_map/sweep_second/pallas_call | solution.py:159
  135.0 0.0 all-to-all-done.2
  135.0 0.0 copy-start
  135.0 1.5 copy-done
  136.6 10.3 %trailing_update.1 = f32[400,800]{1,0:T(8,128)} custom-call(s32[2]{0:T(128)} %pad_add_fusion.1.place_ref, f32[768,400]{1,0:T(8,128)} %all-gather.2.cloned.1.call-done.column_hbm, f32[768,768]{1,0:T(8,128)} %sweep_second.1.inverse_hbm, f32[768,800]{1,0:T(8,128)} %bitcast.7, f32[400,800]{1,0:T(8,128)} %current_hbm.1), custom_call_target="tpu_custom_call" | custom-call | flops 963379200 | bytes 2560000 | tf_op jit(solution)/shard_map/trailing_update/pallas_call | solution.py:237
  (6 shorter events, 0.1 us)
Async XLA Ops:
  40.7 25.0 %slice-start = ((f32[400,800]{1,0:T(8,128)}), f32[24,800]{1,0:T(8,128)S(1)}, s32[]{:S(2)}) async-start(f32[400,800]{1,0:T(8,128)} %current_hbm.1), calls=%async_computation.4 | async-start | bytes 172032 | tf_op jit(solution)/shard_map/slice | solution.py:269
  40.7 20.3 %all-to-all-start.1 = ((f32[16,24,768]{2,1,0:T(8,128)}), f32[16,24,768]{2,1,0:T(8,128)S(1)}, u32[]{:S(2)}, u32[]{:S(2)}) async-start(f32[16,24,768]{2,1,0:T(8,128)} %broadcast_in_dim.10), calls=%async_computation.1 | async-start | bytes 2359296 | tf_op jit(solution)/shard_map/pivot_xy/all_to_all | solution.py:275
  48.3 69.1 %all-gather.2.cloned.1.call-start = ((), (), s32[]{:S(2)}) async-start(), calls=%async_computation.3 | async-start | bytes 1671168 | tf_op jit(solution)/shard_map/column_panel/all_gather | solution.py:279
  61.0 6.6 %copy-start.1 = (f32[16,24,768]{2,1,0:T(8,128)}, f32[16,24,768]{2,1,0:T(8,128)S(1)}, u32[]{:S(2)}) copy-start(f32[16,24,768]{2,1,0:T(8,128)S(1)} %all-to-all-done.1.refs_1_) | copy-start | bytes 3538948
  61.0 4.7 %collective-permute-start = (f32[16,24,768]{2,1,0:T(8,128)S(1)}, f32[16,24,768]{2,1,0:T(8,128)S(1)}, u32[]{:S(2)}, u32[]{:S(2)}) collective-permute-start(f32[16,24,768]{2,1,0:T(8,128)S(1)} %all-to-all-done.1.refs_1_), channel_id=1, source_target_pairs={{0,16},{16,0},{1,17},{17,1},{2,18},{18,2},{3,19},{19,3},{4,20},{20... | collective-permute-start | bytes 3538952 | tf_op jit(solution)/shard_map/pivot_core/ppermute | solution.py:277
  65.8 1.9 %copy-start.2 = (f32[16,24,768]{2,1,0:T(8,128)}, f32[16,24,768]{2,1,0:T(8,128)S(1)}, u32[]{:S(2)}) copy-start(f32[16,24,768]{2,1,0:T(8,128)S(1)} %collective-permute-done.refs_2_) | copy-start | bytes 3538948
  67.7 67.3 %all-to-all-start.2 = ((f32[32,24,800]{2,1,0:T(8,128)}), f32[32,24,800]{2,1,0:T(8,128)S(1)}, u32[]{:S(2)}, u32[]{:S(2)}) async-start(f32[32,24,800]{2,1,0:T(8,128)} %broadcast_in_dim.11), calls=%async_computation.2 | async-start | bytes 5505024 | tf_op jit(solution)/shard_map/row_panel/all_to_all | solution.py:283
  135.0 1.5 %copy-start = (f32[32,24,800]{2,1,0:T(8,128)}, f32[32,24,800]{2,1,0:T(8,128)S(1)}, u32[]{:S(2)}) copy-start(f32[32,24,800]{2,1,0:T(8,128)S(1)} %all-to-all-done.2) | copy-start | bytes 7372804
Sparse Core Ops, SparseCore 0:
  51.3 66.1 all-gather.1

commit v5 on v3

--- a/solution.py
+++ b/solution.py
@@ -133,26 +133,21 @@
     apply_last()
 
 
-def first_kernel(slot_ref, own_ref, other_ref, out_ref, *scratch, last):
-    pairs, band, _ = own_ref.shape
+def inverse_kernel(slot_ref, own_ref, other_ref, out_ref, left_ref, right_ref, diagonal_ref):
+    pairs, band, order = own_ref.shape
     for i in range(pairs):
         out_ref[pl.ds(pl.multiple_of(slot_ref[0, i] * band, 8), band), :] = own_ref[i]
         out_ref[pl.ds(pl.multiple_of(slot_ref[1, i] * band, 8), band), :] = other_ref[i]
-    eliminate(0, last, out_ref, *scratch)
-
-
-def second_kernel(part_ref, out_ref, *scratch, first):
-    out_ref[...] = part_ref[...]
-    eliminate(first, out_ref.shape[0] // TILE, out_ref, *scratch)
-
-
-def pivot_sweep(kernel, order, flops, name, *arrays):
+    eliminate(0, order // TILE, out_ref, left_ref, right_ref, diagonal_ref)
+
+
+def pivot_inverse(slots, own, other):
+    order = own.shape[2]
     vmem = pl.BlockSpec(memory_space=pltpu.VMEM)
-    small = pl.BlockSpec(memory_space=pltpu.SMEM)
     return pl.pallas_call(
-        kernel,
+        inverse_kernel,
         out_shape=jax.ShapeDtypeStruct((order, order), F32),
-        in_specs=[small if array.dtype == jnp.int32 else vmem for array in arrays],
+        in_specs=[pl.BlockSpec(memory_space=pltpu.SMEM), vmem, vmem],
         out_specs=vmem,
         scratch_shapes=[
             pltpu.VMEM((order, 6 * TILE), BF16),
@@ -160,38 +155,47 @@
             pltpu.VMEM((TILE, TILE), F32),
         ],
         compiler_params=pltpu.CompilerParams(vmem_limit_bytes=20 * 1024 * 1024),
-        cost_estimate=pl.CostEstimate(flops=flops, bytes_accessed=8, transcendentals=0),
-        name=name,
-    )(*arrays)
-
-
-def update_kernel(
-    place_ref, column_hbm, inverse_hbm, row_hbm, current_hbm, out_ref,
-    column_ref, inverse_ref, row_ref, current_ref, sems, *, band,
-):
-    sources = (column_hbm, inverse_hbm, row_hbm, current_hbm)
-    targets = (column_ref, inverse_ref, row_ref, current_ref)
+        cost_estimate=pl.CostEstimate(flops=1, bytes_accessed=8, transcendentals=0),
+        name="pivot_inverse",
+    )(slots, own, other)
+
+
+def iota(shape, axis):
+    return lax.broadcasted_iota(jnp.int32, shape, axis)
+
+
+def start_loads(sources, targets, sems):
     loads = [
         pltpu.make_async_copy(source, target, sems.at[i])
         for i, (source, target) in enumerate(zip(sources, targets))
     ]
     for load in loads:
         load.start()
+    return loads
+
+
+def scale_kernel(place_ref, inverse_hbm, column_hbm, out_ref, inverse_ref, column_ref, sems, *, band):
+    loads = start_loads((inverse_hbm, column_hbm), (inverse_ref, column_ref), sems)
+    shape = column_ref.shape
+    loads[0].wait()
+    left = left_parts(inverse_ref[...])
+    pick = jnp.where(iota(shape, 0) == iota(shape, 1) + place_ref[0] * band, -1.0, 0.0)
+    loads[1].wait()
+    column = jnp.where(iota(shape, 1) < band, pick, column_ref[...])
+    out_ref[...] = product(left, right_parts(column)).T
+
+
+def update_kernel(
+    place_ref, row_hbm, scaled_hbm, current_hbm, out_ref,
+    row_ref, scaled_ref, current_ref, sems, *, band,
+):
+    loads = start_loads(
+        (row_hbm, scaled_hbm, current_hbm), (row_ref, scaled_ref, current_ref), sems
+    )
     rows, cols = current_ref.shape
-    order = inverse_ref.shape[0]
+    order = row_ref.shape[0]
     span = rows
-    my_rows = place_ref[0] * band
     my_cols = place_ref[1] * (cols // span) * band
-
-    def iota(shape, axis):
-        return lax.broadcasted_iota(jnp.int32, shape, axis)
-
-    loads[0].wait()
-    shape = (order, rows)
-    pick = jnp.where(iota(shape, 0) == iota(shape, 1) + my_rows, -1.0, 0.0)
-    column = jnp.where(iota(shape, 1) < band, pick, column_ref[...])
-    loads[1].wait()
-    scaled = jnp.dot(inverse_ref[...], column, precision=HIGHEST, preferred_element_type=F32).T
 
     def strip_of(shape):
         at = iota(shape, 1)
@@ -207,42 +211,34 @@
     shape = (order, cols)
     inside, within = strip_of(shape)
     pick = jnp.where(iota(shape, 0) == within + my_cols, -1.0, 0.0)
-    loads[2].wait()
-    row = jnp.where(inside, pick, row_ref[...])
+    loads[0].wait()
+    row_high, row_low, _ = three_parts(jnp.where(inside, pick, row_ref[...]))
+    loads[1].wait()
+    scaled_high, scaled_low, _ = three_parts(scaled_ref[...])
+    change = product(
+        jnp.concatenate([scaled_high, scaled_high, scaled_low], axis=1),
+        jnp.concatenate([row_high, row_low, row_high], axis=0),
+    )
     shape = (rows, cols)
     inside, _ = strip_of(shape)
-    scaled_high, scaled_low, _ = three_parts(scaled)
-    row_high, row_low, _ = three_parts(row)
-    change = product(scaled_high, row_high) + (
-        product(scaled_high, row_low) + product(scaled_low, row_high)
-    )
-    loads[3].wait()
+    loads[2].wait()
     base = jnp.where(inside | (iota(shape, 0) < band), 0.0, current_ref[...])
     out_ref[...] = base - change
 
 
-def trailing_update(place, current, column, row, inverse, band):
-    rows, cols = current.shape
-    order = inverse.shape[0]
+def loading_call(kernel, out_shape, flops, name, place, band, *arrays):
     return pl.pallas_call(
-        functools.partial(update_kernel, band=band),
-        out_shape=jax.ShapeDtypeStruct(current.shape, F32),
+        functools.partial(kernel, band=band),
+        out_shape=jax.ShapeDtypeStruct(out_shape, F32),
         in_specs=[pl.BlockSpec(memory_space=pltpu.SMEM)]
-        + [pl.BlockSpec(memory_space=pl.ANY)] * 4,
+        + [pl.BlockSpec(memory_space=pl.ANY)] * len(arrays),
         out_specs=pl.BlockSpec(memory_space=pltpu.VMEM),
-        scratch_shapes=[
-            pltpu.VMEM(column.shape, F32),
-            pltpu.VMEM(inverse.shape, F32),
-            pltpu.VMEM(row.shape, F32),
-            pltpu.VMEM(current.shape, F32),
-            pltpu.SemaphoreType.DMA((4,)),
-        ],
+        scratch_shapes=[pltpu.VMEM(array.shape, F32) for array in arrays]
+        + [pltpu.SemaphoreType.DMA((len(arrays),))],
         compiler_params=pltpu.CompilerParams(vmem_limit_bytes=56 * 1024 * 1024),
-        cost_estimate=pl.CostEstimate(
-            flops=2 * rows * order * (cols + order), bytes_accessed=8 * rows * cols, transcendentals=0
-        ),
-        name="trailing_update",
-    )(place, column, inverse, row, current)
+        cost_estimate=pl.CostEstimate(flops=flops, bytes_accessed=8, transcendentals=0),
+        name=name,
+    )(place, *arrays)
 
 
 def body(matrix):
@@ -258,10 +254,9 @@
     )
     rowband = matrix[0:band, :]
     with jax.named_scope("pivot_z"):
-        pivot = lax.all_to_all(
-            jnp.broadcast_to(strip[0:band, :], (depth, band, groups * band)), "z", 0, 0
-        )
-    pivot = pivot.transpose(1, 0, 2).reshape(band, K * B)
+        padded = jnp.pad(strip[0:band, :], ((0, 0), (0, TILE - groups * band)))
+        pivot = lax.all_to_all(jnp.broadcast_to(padded, (depth, band, TILE)), "z", 0, 0)
+    pivot = pivot[:, :, : groups * band].transpose(1, 0, 2).reshape(band, K * B)
     with jax.named_scope("pivot_xy"):
         own = lax.all_to_all(jnp.broadcast_to(pivot, (chips, band, K * B)), ("x", "y"), 0, 0)
     with jax.named_scope("pivot_core"):
@@ -275,16 +270,13 @@
     first = 2 * jnp.arange(chips, dtype=jnp.int32)
     slots = jnp.stack([first + core, first + 1 - core])
     order = K * B
-    half = 2
-    part = pivot_sweep(
-        functools.partial(first_kernel, last=half), order, 1, "sweep_first", slots, own, other
-    )
-    column, part = lax.optimization_barrier((column, part))
-    inverse = pivot_sweep(
-        functools.partial(second_kernel, first=half), order, 10**12, "sweep_second", part
-    )
-    return trailing_update(
-        place, matrix, column, row.reshape(K * B, cols), inverse, band
+    inverse = pivot_inverse(slots, own, other)
+    scaled = loading_call(
+        scale_kernel, (rows, order), 24*10**9, "scale", place, band, inverse, column
+    )
+    row = row.reshape(order, cols)
+    return loading_call(
+        update_kernel, (rows, cols), 1, "trailing_update", place, band, row, scaled, matrix
     )
 
 

time: 162 us -> 142 us (0.88)
  the two profiles are of different devices: /device:TPU:1 before, /device:TPU:39 now
where the time goes in v5:
time: 142 us
  Pallas kernels  54.9 us (39%)
  blocking collectives  30.3 us (21%)
  starting transfers between devices  18.7 us (13%)
  waiting for transfers between devices  16.9 us (12%)
  between operations  13.5 us (10%)
  local copies, waits for them, and re-layouts  5.89 us (4%)
    pallas_call x1, Pallas kernels, pivot_inverse(): pl.pallas_call(inverse_kernel, out_shape=jax.ShapeDtypeStruct((order, ord...  40.4 us
    all_to_all x1, blocking collectives, body(): lax.all_to_all(jnp.broadcast_to(padded, (depth, band, TILE)), 'z', 0, 0)  30.3 us
    pallas_call x2, Pallas kernels, loading_call(): pl.pallas_call(functools.partial(kernel, band=band), out_shape=jax.ShapeD...  14.6 us
    all_to_all x1, waiting for transfers between devices, body(): lax.all_to_all(jnp.broadcast_to(pivot, (chips, band, K * B)), ('x', 'y'),...  14.4 us
    all_to_all x1, starting transfers between devices, body(): row = lax.all_to_all(spread, ('x', 'y', 'c'), 0, 0)  7.03 us
    all_to_all x1, starting transfers between devices, body(): lax.all_to_all(jnp.broadcast_to(pivot, (chips, band, K * B)), ('x', 'y'),...  7 us
    ppermute x1, starting transfers between devices, body(): other = lax.ppermute(own, 'c', [(0, 1), (1, 0)])  4.67 us
  transfers between devices with their start and end apart: 4, of which 2 were waited for; matrix products, arithmetic and copies ran while one was open for 2% of the time, Pallas kernels for 34%

profile of v5, /device:TPU:39, one launch (start us, length us, event | category | flops | bytes accessed | tf_op | source)
XLA Modules:
  0.0 141.6 jit_solution(12075565558695050332)
XLA Ops:
  6.5 1.1 fusion.3
  7.7 0.1 copy.12
  7.8 0.1 copy.13
  7.9 0.1 copy.14
  8.0 30.3 %all_to_all.15 = f32[16,24,128]{2,1,0:T(8,128)S(1)} all-to-all(f32[16,24,128]{2,1,0:T(8,128)S(1)} %broadcast_in_dim.10), channel_id=1, replica_groups=mesh['x'=4,'y'=4,'c'=2,'z'=16] {'z'}, dimensions={0} | all-to-all | bytes 393216 | tf_op jit(solution)/shard_map/pivot_z/all_to_all | solution.py:258
  38.4 0.1 reshape.23
  38.5 1.1 broadcast_in_dim.11
  39.6 0.0 slice-start
  39.6 7.0 %all-to-all-start.1 = ((f32[16,24,768]{2,1,0:T(8,128)}), f32[16,24,768]{2,1,0:T(8,128)S(1)}, u32[]{:S(2)}, u32[]{:S(2)}) async-start(f32[16,24,768]{2,1,0:T(8,128)} %broadcast_in_dim.11), calls=%async_computation.1 | async-start | bytes 2359296 | tf_op jit(solution)/shard_map/pivot_xy/all_to_all | solution.py:261
  46.6 0.0 all-gather.2.cloned.1.call-start
  46.7 0.6 fusion
  47.3 0.0 all-gather.2.cloned.1.call-update
  47.4 14.4 %all-to-all-done.1.own_ref = f32[16,24,768]{2,1,0:T(8,128)S(1)} async-done(((f32[16,24,768]{2,1,0:T(8,128)}), f32[16,24,768]{2,1,0:T(8,128)S(1)}, u32[]{:S(2)}, u32[]{:S(2)}) %all-to-all-start.1) | async-done | bytes 1179680 | tf_op jit(solution)/shard_map/pivot_xy/all_to_all | solution.py:261
  61.8 4.7 %collective-permute-start = (f32[16,24,768]{2,1,0:T(8,128)S(1)}, f32[16,24,768]{2,1,0:T(8,128)S(1)}, u32[]{:S(2)}, u32[]{:S(2)}) collective-permute-start(f32[16,24,768]{2,1,0:T(8,128)S(1)} %all-to-all-done.1.own_ref), channel_id=1, source_target_pairs={{0,16},{16,0},{1,17},{17,1},{2,18},{18,2},{3,19},{19,3},{4,20},{20... | collective-permute-start | bytes 3538952 | tf_op jit(solution)/shard_map/pivot_core/ppermute | solution.py:263
  66.5 2.4 %collective-permute-done.other_ref = f32[16,24,768]{2,1,0:T(8,128)S(1)} collective-permute-done((f32[16,24,768]{2,1,0:T(8,128)S(1)}, f32[16,24,768]{2,1,0:T(8,128)S(1)}, u32[]{:S(2)}, u32[]{:S(2)}) %collective-permute-start) | collective-permute-done | bytes 1179680 | tf_op jit(solution)/shard_map/pivot_core/ppermute | solution.py:263
  68.9 0.0 slice-done
  68.9 1.8 %broadcast_in_dim.9 = f32[32,24,800]{2,1,0:T(8,128)} broadcast(f32[24,800]{1,0:T(8,128)S(1)} %slice-done), dimensions={1,2} | broadcast | bytes 2534400 | tf_op jit(solution)/shard_map/broadcast_in_dim | solution.py:266
  70.7 7.0 %all-to-all-start.2 = ((f32[32,24,800]{2,1,0:T(8,128)}), f32[32,24,800]{2,1,0:T(8,128)}, u32[]{:S(2)}, u32[]{:S(2)}) async-start(f32[32,24,800]{2,1,0:T(8,128)} %broadcast_in_dim.9), calls=%async_computation.2 | async-start | bytes 5505024 | tf_op jit(solution)/shard_map/row_panel/all_to_all | solution.py:269
  77.7 0.6 pad_add_fusion.1.place_ref
  78.3 40.4 %pivot_inverse.1.inverse_hbm = f32[768,768]{1,0:T(8,128)S(1)} custom-call(s32[2,16]{1,0:T(2,128)S(1)} %pad_add_fusion.slot_ref, f32[16,24,768]{2,1,0:T(8,128)S(1)} %all-to-all-done.1.own_ref, f32[16,24,768]{2,1,0:T(8,128)S(1)} %collective-permute-done.other_ref), custom_call_target="tpu_custom_call" | custom-call | flops 1 | bytes 8 | tf_op jit(solution)/shard_map/pivot_inverse/pallas_call | solution.py:147
  118.7 0.0 copy-start
  118.7 1.4 copy-done
  120.1 0.0 all-gather.2.cloned.1.call-done.column_hbm
  120.1 8.3 %scale.1.scaled_hbm = f32[400,768]{1,0:T(8,128)} custom-call(s32[2]{0:T(128)} %pad_add_fusion.1.place_ref, f32[768,768]{1,0:T(8,128)} %copy-done, f32[768,400]{1,0:T(8,128)} %all-gather.2.cloned.1.call-done.column_hbm), custom_call_target="tpu_custom_call" | custom-call | flops 24000000000 | bytes 8 | tf_op jit(solution)/shard_map/scale/pallas_call | solution.py:230
  128.4 0.0 all-to-all-done.2
  128.4 6.3 %trailing_update.1 = f32[400,800]{1,0:T(8,128)} custom-call(s32[2]{0:T(128)} %pad_add_fusion.1.place_ref, f32[768,800]{1,0:T(8,128)} %bitcast.3.row_hbm, f32[400,768]{1,0:T(8,128)} %scale.1.scaled_hbm, f32[400,800]{1,0:T(8,128)} %current_hbm.1), custom_call_target="tpu_custom_call" | custom-call | flops 1 | bytes 8 | tf_op jit(solution)/shard_map/trailing_update/pallas_call | solution.py:230
  (7 shorter events, 0.1 us)
Async XLA Ops:
  39.6 29.3 %slice-start = ((f32[400,800]{1,0:T(8,128)}), f32[24,800]{1,0:T(8,128)S(1)}, s32[]{:S(2)}) async-start(f32[400,800]{1,0:T(8,128)} %current_hbm.1), calls=%async_computation.4 | async-start | bytes 172032 | tf_op jit(solution)/shard_map/slice | solution.py:255
  39.6 22.2 %all-to-all-start.1 = ((f32[16,24,768]{2,1,0:T(8,128)}), f32[16,24,768]{2,1,0:T(8,128)S(1)}, u32[]{:S(2)}, u32[]{:S(2)}) async-start(f32[16,24,768]{2,1,0:T(8,128)} %broadcast_in_dim.11), calls=%async_computation.1 | async-start | bytes 2359296 | tf_op jit(solution)/shard_map/pivot_xy/all_to_all | solution.py:261
  46.6 73.5 %all-gather.2.cloned.1.call-start = ((), (), s32[]{:S(2)}) async-start(), calls=%async_computation.3 | async-start | bytes 1671168 | tf_op jit(solution)/shard_map/column_panel/all_gather | solution.py:265
  61.8 7.1 %collective-permute-start = (f32[16,24,768]{2,1,0:T(8,128)S(1)}, f32[16,24,768]{2,1,0:T(8,128)S(1)}, u32[]{:S(2)}, u32[]{:S(2)}) collective-permute-start(f32[16,24,768]{2,1,0:T(8,128)S(1)} %all-to-all-done.1.own_ref), channel_id=1, source_target_pairs={{0,16},{16,0},{1,17},{17,1},{2,18},{18,2},{3,19},{19,3},{4,20},{20... | collective-permute-start | bytes 3538952 | tf_op jit(solution)/shard_map/pivot_core/ppermute | solution.py:263
  70.7 57.7 %all-to-all-start.2 = ((f32[32,24,800]{2,1,0:T(8,128)}), f32[32,24,800]{2,1,0:T(8,128)}, u32[]{:S(2)}, u32[]{:S(2)}) async-start(f32[32,24,800]{2,1,0:T(8,128)} %broadcast_in_dim.9), calls=%async_computation.2 | async-start | bytes 5505024 | tf_op jit(solution)/shard_map/row_panel/all_to_all | solution.py:269
  118.7 1.4 copy-start
Sparse Core Ops, SparseCore 0:
  49.5 58.6 all-gather.1

commit v6 on v5

--- a/solution.py
+++ b/solution.py
@@ -178,11 +178,11 @@
     loads = start_loads((inverse_hbm, column_hbm), (inverse_ref, column_ref), sems)
     shape = column_ref.shape
     loads[0].wait()
-    left = left_parts(inverse_ref[...])
+    right = right_parts(inverse_ref[...])
     pick = jnp.where(iota(shape, 0) == iota(shape, 1) + place_ref[0] * band, -1.0, 0.0)
     loads[1].wait()
     column = jnp.where(iota(shape, 1) < band, pick, column_ref[...])
-    out_ref[...] = product(left, right_parts(column)).T
+    out_ref[...] = product(left_parts(column.T), right)
 
 
 def update_kernel(
@@ -259,12 +259,12 @@
     pivot = pivot[:, :, : groups * band].transpose(1, 0, 2).reshape(band, K * B)
     with jax.named_scope("pivot_xy"):
         own = lax.all_to_all(jnp.broadcast_to(pivot, (chips, band, K * B)), ("x", "y"), 0, 0)
-    with jax.named_scope("pivot_core"):
-        other = lax.ppermute(own, "c", [(0, 1), (1, 0)])
     with jax.named_scope("column_panel"):
         column = lax.all_gather(strip.T, "z", axis=0, tiled=True)
     spread = jnp.broadcast_to(rowband, (2 * chips, band, cols))
-    spread, other = lax.optimization_barrier((spread, other))
+    spread, own = lax.optimization_barrier((spread, own))
+    with jax.named_scope("pivot_core"):
+        other = lax.ppermute(own, "c", [(0, 1), (1, 0)])
     with jax.named_scope("row_panel"):
         row = lax.all_to_all(spread, ("x", "y", "c"), 0, 0)
     first = 2 * jnp.arange(chips, dtype=jnp.int32)

time: 142 us -> 139 us (0.979)
  blocking collectives: 30.3 us -> 0 us
  starting transfers between devices: 18.7 us -> 33 us
  waiting for transfers between devices: 16.9 us -> 30.3 us
    all_to_all x1 -> x0, blocking collectives: 30.3 us -> none  [body(): lax.all_to_all(jnp.broadcast_to(padded, (depth, band, TILE)), 'z', 0, 0)]
    all_to_all x0 -> x1, waiting for transfers between devices: none -> 15.1 us  [body(): lax.all_to_all(jnp.broadcast_to(padded, (depth, band, TILE)), 'z', 0, 0)]
    all_to_all x0 -> x1, starting transfers between devices: none -> 14.7 us  [body(): lax.all_to_all(jnp.broadcast_to(padded, (depth, band, TILE)), 'z', 0, 0)]
    ppermute x1, waiting for transfers between devices: 2.43 us -> 0.01 us  [body(): other = lax.ppermute(own, 'c', [(0, 1), (1, 0)])]
  transfers between devices with their start and end apart: 4 -> 5, of which waited for: 2 -> 2; matrix products, arithmetic and copies ran while one was open for 2% -> 3% of each run, Pallas kernels for 34% -> 34%
where the time goes in v6:
time: 139 us
  Pallas kernels  53.9 us (39%)
  starting transfers between devices  33 us (24%)
  waiting for transfers between devices  30.3 us (22%)
  between operations  13.5 us (10%)
  local copies, waits for them, and re-layouts  6.51 us (5%)
    pallas_call x1, Pallas kernels, pivot_inverse(): pl.pallas_call(inverse_kernel, out_shape=jax.ShapeDtypeStruct((order, ord...  40.4 us
    all_to_all x1, waiting for transfers between devices, body(): lax.all_to_all(jnp.broadcast_to(pivot, (chips, band, K * B)), ('x', 'y'),...  15.2 us
    all_to_all x1, waiting for transfers between devices, body(): lax.all_to_all(jnp.broadcast_to(padded, (depth, band, TILE)), 'z', 0, 0)  15.1 us
    all_to_all x1, starting transfers between devices, body(): lax.all_to_all(jnp.broadcast_to(padded, (depth, band, TILE)), 'z', 0, 0)  14.7 us
    pallas_call x2, Pallas kernels, loading_call(): pl.pallas_call(functools.partial(kernel, band=band), out_shape=jax.ShapeD...  13.6 us
    all_to_all x1, starting transfers between devices, body(): lax.all_to_all(jnp.broadcast_to(pivot, (chips, band, K * B)), ('x', 'y'),...  7 us
    all_to_all x1, starting transfers between devices, body(): row = lax.all_to_all(spread, ('x', 'y', 'c'), 0, 0)  6.69 us
    ppermute x1, starting transfers between devices, body(): other = lax.ppermute(own, 'c', [(0, 1), (1, 0)])  4.67 us
  transfers between devices with their start and end apart: 5, of which 2 were waited for; matrix products, arithmetic and copies ran while one was open for 3% of the time, Pallas kernels for 34%

profile of v6, /device:TPU:39, one launch (start us, length us, event | category | flops | bytes accessed | tf_op | source)
XLA Modules:
  0.0 138.7 jit_solution(4074957695470719281)
XLA Ops:
  6.5 1.1 fusion.3
  7.7 0.1 copy.12
  7.8 0.1 copy.13
  7.9 0.1 copy.14
  8.0 0.7 broadcast_in_dim.10
  8.7 14.7 %all-to-all-start = ((f32[16,24,128]{2,1,0:T(8,128)}), f32[16,24,128]{2,1,0:T(8,128)S(1)}, u32[]{:S(2)}, u32[]{:S(2)}) async-start(f32[16,24,128]{2,1,0:T(8,128)} %broadcast_in_dim.10), calls=%async_computation | async-start | bytes 393216 | tf_op jit(solution)/shard_map/pivot_z/all_to_all | solution.py:258
  23.3 0.0 all-gather.2.cloned.1.call-start
  23.4 0.7 fusion
  24.0 0.0 all-gather.2.cloned.1.call-update
  24.1 15.1 %all-to-all-done = f32[16,24,128]{2,1,0:T(8,128)S(1)} async-done(((f32[16,24,128]{2,1,0:T(8,128)}), f32[16,24,128]{2,1,0:T(8,128)S(1)}, u32[]{:S(2)}, u32[]{:S(2)}) %all-to-all-start) | async-done | bytes 196640 | tf_op jit(solution)/shard_map/pivot_z/all_to_all | solution.py:258
  39.3 0.1 reshape.23
  39.4 1.1 broadcast_in_dim.11
  40.5 0.0 slice-start
  40.5 7.0 %all-to-all-start.1 = ((f32[16,24,768]{2,1,0:T(8,128)}), f32[16,24,768]{2,1,0:T(8,128)S(1)}, u32[]{:S(2)}, u32[]{:S(2)}) async-start(f32[16,24,768]{2,1,0:T(8,128)} %broadcast_in_dim.11), calls=%async_computation.1 | async-start | bytes 2359296 | tf_op jit(solution)/shard_map/pivot_xy/all_to_all | solution.py:261
  47.5 15.2 %all-to-all-done.1.own_ref = f32[16,24,768]{2,1,0:T(8,128)S(1)} async-done(((f32[16,24,768]{2,1,0:T(8,128)}), f32[16,24,768]{2,1,0:T(8,128)S(1)}, u32[]{:S(2)}, u32[]{:S(2)}) %all-to-all-start.1) | async-done | bytes 1179680 | tf_op jit(solution)/shard_map/pivot_xy/all_to_all | solution.py:261
  62.7 0.0 slice-done
  62.7 1.7 %broadcast_in_dim.9 = f32[32,24,800]{2,1,0:T(8,128)} broadcast(f32[24,800]{1,0:T(8,128)S(1)} %slice-done), dimensions={1,2} | broadcast | bytes 2534400 | tf_op jit(solution)/shard_map/broadcast_in_dim | solution.py:264
  64.4 4.7 %collective-permute-start = (f32[16,24,768]{2,1,0:T(8,128)S(1)}, f32[16,24,768]{2,1,0:T(8,128)S(1)}, u32[]{:S(2)}, u32[]{:S(2)}) collective-permute-start(f32[16,24,768]{2,1,0:T(8,128)S(1)} %all-to-all-done.1.own_ref), channel_id=1, source_target_pairs={{0,16},{16,0},{1,17},{17,1},{2,18},{18,2},{3,19},{19,3},{4,20},{20... | collective-permute-start | bytes 3538952 | tf_op jit(solution)/shard_map/pivot_core/ppermute | solution.py:267
  69.1 6.7 %all-to-all-start.2 = ((f32[32,24,800]{2,1,0:T(8,128)}), f32[32,24,800]{2,1,0:T(8,128)}, u32[]{:S(2)}, u32[]{:S(2)}) async-start(f32[32,24,800]{2,1,0:T(8,128)} %broadcast_in_dim.9), calls=%async_computation.2 | async-start | bytes 5505024 | tf_op jit(solution)/shard_map/row_panel/all_to_all | solution.py:269
  75.8 0.7 pad_add_fusion.1.place_ref
  76.5 0.0 collective-permute-done.other_ref
  76.5 40.4 %pivot_inverse.1.inverse_hbm = f32[768,768]{1,0:T(8,128)S(1)} custom-call(s32[2,16]{1,0:T(2,128)S(1)} %pad_add_fusion.slot_ref, f32[16,24,768]{2,1,0:T(8,128)S(1)} %all-to-all-done.1.own_ref, f32[16,24,768]{2,1,0:T(8,128)S(1)} %collective-permute-done.other_ref), custom_call_target="tpu_custom_call" | custom-call | flops 1 | bytes 8 | tf_op jit(solution)/shard_map/pivot_inverse/pallas_call | solution.py:147
  116.9 0.0 copy-start
  116.9 1.4 copy-done
  118.3 0.0 all-gather.2.cloned.1.call-done.column_hbm
  118.3 7.3 %scale.1.scaled_hbm = f32[400,768]{1,0:T(8,128)} custom-call(s32[2]{0:T(128)} %pad_add_fusion.1.place_ref, f32[768,768]{1,0:T(8,128)} %copy-done, f32[768,400]{1,0:T(8,128)} %all-gather.2.cloned.1.call-done.column_hbm), custom_call_target="tpu_custom_call" | custom-call | flops 24000000000 | bytes 8 | tf_op jit(solution)/shard_map/scale/pallas_call | solution.py:230
  125.6 0.0 all-to-all-done.2
  125.6 6.3 %trailing_update.1 = f32[400,800]{1,0:T(8,128)} custom-call(s32[2]{0:T(128)} %pad_add_fusion.1.place_ref, f32[768,800]{1,0:T(8,128)} %bitcast.3.row_hbm, f32[400,768]{1,0:T(8,128)} %scale.1.scaled_hbm, f32[400,800]{1,0:T(8,128)} %current_hbm.1), custom_call_target="tpu_custom_call" | custom-call | flops 1 | bytes 8 | tf_op jit(solution)/shard_map/trailing_update/pallas_call | solution.py:230
  (6 shorter events, 0.1 us)
Async XLA Ops:
  8.7 30.5 %all-to-all-start = ((f32[16,24,128]{2,1,0:T(8,128)}), f32[16,24,128]{2,1,0:T(8,128)S(1)}, u32[]{:S(2)}, u32[]{:S(2)}) async-start(f32[16,24,128]{2,1,0:T(8,128)} %broadcast_in_dim.10), calls=%async_computation | async-start | bytes 393216 | tf_op jit(solution)/shard_map/pivot_z/all_to_all | solution.py:258
  23.3 94.9 %all-gather.2.cloned.1.call-start = ((), (), s32[]{:S(2)}) async-start(), calls=%async_computation.3 | async-start | bytes 1671168 | tf_op jit(solution)/shard_map/column_panel/all_gather | solution.py:263
  40.5 22.2 %slice-start = ((f32[400,800]{1,0:T(8,128)}), f32[24,800]{1,0:T(8,128)S(1)}, s32[]{:S(2)}) async-start(f32[400,800]{1,0:T(8,128)} %current_hbm.1), calls=%async_computation.4 | async-start | bytes 172032 | tf_op jit(solution)/shard_map/slice | solution.py:255
  40.5 22.2 %all-to-all-start.1 = ((f32[16,24,768]{2,1,0:T(8,128)}), f32[16,24,768]{2,1,0:T(8,128)S(1)}, u32[]{:S(2)}, u32[]{:S(2)}) async-start(f32[16,24,768]{2,1,0:T(8,128)} %broadcast_in_dim.11), calls=%async_computation.1 | async-start | bytes 2359296 | tf_op jit(solution)/shard_map/pivot_xy/all_to_all | solution.py:261
  64.4 12.1 %collective-permute-start = (f32[16,24,768]{2,1,0:T(8,128)S(1)}, f32[16,24,768]{2,1,0:T(8,128)S(1)}, u32[]{:S(2)}, u32[]{:S(2)}) collective-permute-start(f32[16,24,768]{2,1,0:T(8,128)S(1)} %all-to-all-done.1.own_ref), channel_id=1, source_target_pairs={{0,16},{16,0},{1,17},{17,1},{2,18},{18,2},{3,19},{19,3},{4,20},{20... | collective-permute-start | bytes 3538952 | tf_op jit(solution)/shard_map/pivot_core/ppermute | solution.py:267
  69.1 56.5 %all-to-all-start.2 = ((f32[32,24,800]{2,1,0:T(8,128)}), f32[32,24,800]{2,1,0:T(8,128)}, u32[]{:S(2)}, u32[]{:S(2)}) async-start(f32[32,24,800]{2,1,0:T(8,128)} %broadcast_in_dim.9), calls=%async_computation.2 | async-start | bytes 5505024 | tf_op jit(solution)/shard_map/row_panel/all_to_all | solution.py:269
  116.9 1.4 %copy-start = (f32[768,768]{1,0:T(8,128)}, f32[768,768]{1,0:T(8,128)S(1)}, u32[]{:S(2)}) copy-start(f32[768,768]{1,0:T(8,128)S(1)} %pivot_inverse.1.inverse_hbm) | copy-start | bytes 7077892
Sparse Core Ops, SparseCore 0:
  26.3 64.8 all-gather.1

commit v7 on v6

--- a/solution.py
+++ b/solution.py
@@ -107,8 +107,9 @@
     right_ref[...] = jnp.zeros(right_ref.shape, BF16)
 
     def apply_last():
-        for c in range(blocks):
-            here = slice(TILE * c, TILE * c + TILE)
+        wide = 2 * TILE
+        for c in range(order // wide):
+            here = slice(wide * c, wide * c + wide)
             out_ref[:, here] = out_ref[:, here] - product(left_ref[...], right_ref[:, here])
 
     def step(k, carry):
@@ -259,9 +260,10 @@
     pivot = pivot[:, :, : groups * band].transpose(1, 0, 2).reshape(band, K * B)
     with jax.named_scope("pivot_xy"):
         own = lax.all_to_all(jnp.broadcast_to(pivot, (chips, band, K * B)), ("x", "y"), 0, 0)
+    spread = jnp.broadcast_to(rowband, (2 * chips, band, cols))
+    turned, spread = lax.optimization_barrier((strip.T, spread))
     with jax.named_scope("column_panel"):
-        column = lax.all_gather(strip.T, "z", axis=0, tiled=True)
-    spread = jnp.broadcast_to(rowband, (2 * chips, band, cols))
+        column = lax.all_gather(turned, "z", axis=0, tiled=True)
     spread, own = lax.optimization_barrier((spread, own))
     with jax.named_scope("pivot_core"):
         other = lax.ppermute(own, "c", [(0, 1), (1, 0)])

time: 139 us -> 133 us (0.957)
  blocking collectives: 0 us -> 21.7 us
  waiting for transfers between devices: 30.3 us -> 13.5 us
  starting transfers between devices: 33 us -> 25.4 us
  Pallas kernels: 53.9 us -> 52 us
    all_to_all x0 -> x1, blocking collectives: none -> 21.7 us  [body(): lax.all_to_all(jnp.broadcast_to(pivot, (chips, band, K * B)), ('x', 'y'),...]
    all_to_all x1 -> x0, waiting for transfers between devices: 15.2 us -> none  [body(): lax.all_to_all(jnp.broadcast_to(pivot, (chips, band, K * B)), ('x', 'y'),...]
    all_to_all x1 -> x0, starting transfers between devices: 7 us -> none  [body(): lax.all_to_all(jnp.broadcast_to(pivot, (chips, band, K * B)), ('x', 'y'),...]
    pallas_call x1, Pallas kernels: 40.4 us -> 38.5 us  [pivot_inverse(): pl.pallas_call(inverse_kernel, out_shape=jax.ShapeDtypeStruct((order, ord...]
    all_to_all x1, waiting for transfers between devices: 15.1 us -> 13.4 us  [body(): lax.all_to_all(jnp.broadcast_to(padded, (depth, band, TILE)), 'z', 0, 0)]
  transfers between devices with their start and end apart: 5 -> 4, of which waited for: 2 -> 1; matrix products, arithmetic and copies ran while one was open for 3% -> 2% of each run, Pallas kernels for 34% -> 34%
where the time goes in v7:
time: 133 us
  Pallas kernels  52 us (39%)
  starting transfers between devices  25.4 us (19%)
  blocking collectives  21.7 us (16%)
  waiting for transfers between devices  13.5 us (10%)
  between operations  13.5 us (10%)
  local copies, waits for them, and re-layouts  5.53 us (4%)
    pallas_call x1, Pallas kernels, pivot_inverse(): pl.pallas_call(inverse_kernel, out_shape=jax.ShapeDtypeStruct((order, ord...  38.5 us
    all_to_all x1, blocking collectives, body(): lax.all_to_all(jnp.broadcast_to(pivot, (chips, band, K * B)), ('x', 'y'),...  21.7 us
    all_to_all x1, starting transfers between devices, body(): lax.all_to_all(jnp.broadcast_to(padded, (depth, band, TILE)), 'z', 0, 0)  14.7 us
    pallas_call x2, Pallas kernels, loading_call(): pl.pallas_call(functools.partial(kernel, band=band), out_shape=jax.ShapeD...  13.6 us
    all_to_all x1, waiting for transfers between devices, body(): lax.all_to_all(jnp.broadcast_to(padded, (depth, band, TILE)), 'z', 0, 0)  13.4 us
    all_to_all x1, starting transfers between devices, body(): row = lax.all_to_all(spread, ('x', 'y', 'c'), 0, 0)  6.29 us
    ppermute x1, starting transfers between devices, body(): other = lax.ppermute(own, 'c', [(0, 1), (1, 0)])  4.44 us
  transfers between devices with their start and end apart: 4, of which 1 were waited for; matrix products, arithmetic and copies ran while one was open for 2% of the time, Pallas kernels for 34%

profile of v7, /device:TPU:39, one launch (start us, length us, event | category | flops | bytes accessed | tf_op | source)
XLA Modules:
  0.0 133.0 jit_solution(5855402787132377529)
XLA Ops:
  6.5 0.0 slice-start
  6.5 1.2 fusion.3
  7.7 0.1 copy.13
  7.8 0.1 copy.12
  7.9 0.1 copy.14
  8.0 0.7 broadcast_in_dim.10
  8.7 14.7 %all-to-all-start = ((f32[16,24,128]{2,1,0:T(8,128)}), f32[16,24,128]{2,1,0:T(8,128)S(1)}, u32[]{:S(2)}, u32[]{:S(2)}) async-start(f32[16,24,128]{2,1,0:T(8,128)} %broadcast_in_dim.10), calls=%async_computation | async-start | bytes 393216 | tf_op jit(solution)/shard_map/pivot_z/all_to_all | solution.py:259
  23.4 0.0 all-gather.2.cloned.1.call-start
  23.4 0.6 fusion
  24.1 0.0 slice-done
  24.1 1.7 %broadcast_in_dim.9 = f32[32,24,800]{2,1,0:T(8,128)} broadcast(f32[24,800]{1,0:T(8,128)S(1)} %slice-done), dimensions={1,2} | broadcast | bytes 2534400 | tf_op jit(solution)/shard_map/broadcast_in_dim | solution.py:263
  25.8 0.0 all-gather.2.cloned.1.call-update
  25.8 13.4 %all-to-all-done = f32[16,24,128]{2,1,0:T(8,128)S(1)} async-done(((f32[16,24,128]{2,1,0:T(8,128)}), f32[16,24,128]{2,1,0:T(8,128)S(1)}, u32[]{:S(2)}, u32[]{:S(2)}) %all-to-all-start) | async-done | bytes 196640 | tf_op jit(solution)/shard_map/pivot_z/all_to_all | solution.py:259
  39.3 0.1 reshape.23
  39.4 0.1 broadcast_in_dim.11
  39.5 21.7 %all_to_all.15.own_ref = f32[16,24,768]{2,1,0:T(8,128)S(1)} all-to-all(f32[16,24,768]{2,1,0:T(8,128)S(1)} %broadcast_in_dim.11), channel_id=1, replica_groups=mesh['x'=4,'y'=4,'c'=2,'z'=16] {'x','y'}, dimensions={0} | all-to-all | bytes 2359296 | tf_op jit(solution)/shard_map/pivot_xy/all_to_all | solution.py:262
  61.3 4.4 %collective-permute-start = (f32[16,24,768]{2,1,0:T(8,128)S(1)}, f32[16,24,768]{2,1,0:T(8,128)S(1)}, u32[]{:S(2)}, u32[]{:S(2)}) collective-permute-start(f32[16,24,768]{2,1,0:T(8,128)S(1)} %all_to_all.15.own_ref), channel_id=1, source_target_pairs={{0,16},{16,0},{1,17},{17,1},{2,18},{18,2},{3,19},{19,3},{4,20},{20... | collective-permute-start | bytes 3538952 | tf_op jit(solution)/shard_map/pivot_core/ppermute | solution.py:269
  65.7 6.3 %all-to-all-start.2 = ((f32[32,24,800]{2,1,0:T(8,128)}), f32[32,24,800]{2,1,0:T(8,128)}, u32[]{:S(2)}, u32[]{:S(2)}) async-start(f32[32,24,800]{2,1,0:T(8,128)} %broadcast_in_dim.9), calls=%async_computation.2 | async-start | bytes 5505024 | tf_op jit(solution)/shard_map/row_panel/all_to_all | solution.py:271
  72.0 0.6 pad_add_fusion.1.place_ref
  72.6 0.0 collective-permute-done.other_ref
  72.6 38.5 %pivot_inverse.1.inverse_hbm = f32[768,768]{1,0:T(8,128)S(1)} custom-call(s32[2,16]{1,0:T(2,128)S(1)} %pad_add_fusion.slot_ref, f32[16,24,768]{2,1,0:T(8,128)S(1)} %all_to_all.15.own_ref, f32[16,24,768]{2,1,0:T(8,128)S(1)} %collective-permute-done.other_ref), custom_call_target="tpu_custom_call" | custom-call | flops 1 | bytes 8 | tf_op jit(solution)/shard_map/pivot_inverse/pallas_call | solution.py:148
  111.1 0.0 copy-start
  111.1 1.4 %copy-done = f32[768,768]{1,0:T(8,128)} copy-done((f32[768,768]{1,0:T(8,128)}, f32[768,768]{1,0:T(8,128)S(1)}, u32[]{:S(2)}) %copy-start) | copy-done | bytes 2359320
  112.5 0.0 all-gather.2.cloned.1.call-done.column_hbm
  112.5 7.3 %scale.1.scaled_hbm = f32[400,768]{1,0:T(8,128)} custom-call(s32[2]{0:T(128)} %pad_add_fusion.1.place_ref, f32[768,768]{1,0:T(8,128)} %copy-done, f32[768,400]{1,0:T(8,128)} %all-gather.2.cloned.1.call-done.column_hbm), custom_call_target="tpu_custom_call" | custom-call | flops 24000000000 | bytes 8 | tf_op jit(solution)/shard_map/scale/pallas_call | solution.py:231
  119.8 0.0 all-to-all-done.2
  119.9 6.3 %trailing_update.1 = f32[400,800]{1,0:T(8,128)} custom-call(s32[2]{0:T(128)} %pad_add_fusion.1.place_ref, f32[768,800]{1,0:T(8,128)} %bitcast.4.row_hbm, f32[400,768]{1,0:T(8,128)} %scale.1.scaled_hbm, f32[400,800]{1,0:T(8,128)} %current_hbm.1), custom_call_target="tpu_custom_call" | custom-call | flops 1 | bytes 8 | tf_op jit(solution)/shard_map/trailing_update/pallas_call | solution.py:231
  (6 shorter events, 0.1 us)
Async XLA Ops:
  6.5 17.5 %slice-start = ((f32[400,800]{1,0:T(8,128)}), f32[24,800]{1,0:T(8,128)S(1)}, s32[]{:S(2)}) async-start(f32[400,800]{1,0:T(8,128)} %current_hbm.1), calls=%async_computation.4 | async-start | bytes 172032 | tf_op jit(solution)/shard_map/slice | solution.py:256
  8.7 30.5 %all-to-all-start = ((f32[16,24,128]{2,1,0:T(8,128)}), f32[16,24,128]{2,1,0:T(8,128)S(1)}, u32[]{:S(2)}, u32[]{:S(2)}) async-start(f32[16,24,128]{2,1,0:T(8,128)} %broadcast_in_dim.10), calls=%async_computation | async-start | bytes 393216 | tf_op jit(solution)/shard_map/pivot_z/all_to_all | solution.py:259
  23.4 89.1 %all-gather.2.cloned.1.call-start = ((), (), s32[]{:S(2)}) async-start(), calls=%async_computation.3 | async-start | bytes 1671168 | tf_op jit(solution)/shard_map/column_panel/all_gather | solution.py:266
  61.3 11.4 %collective-permute-start = (f32[16,24,768]{2,1,0:T(8,128)S(1)}, f32[16,24,768]{2,1,0:T(8,128)S(1)}, u32[]{:S(2)}, u32[]{:S(2)}) collective-permute-start(f32[16,24,768]{2,1,0:T(8,128)S(1)} %all_to_all.15.own_ref), channel_id=1, source_target_pairs={{0,16},{16,0},{1,17},{17,1},{2,18},{18,2},{3,19},{19,3},{4,20},{20... | collective-permute-start | bytes 3538952 | tf_op jit(solution)/shard_map/pivot_core/ppermute | solution.py:269
  65.7 54.1 %all-to-all-start.2 = ((f32[32,24,800]{2,1,0:T(8,128)}), f32[32,24,800]{2,1,0:T(8,128)}, u32[]{:S(2)}, u32[]{:S(2)}) async-start(f32[32,24,800]{2,1,0:T(8,128)} %broadcast_in_dim.9), calls=%async_computation.2 | async-start | bytes 5505024 | tf_op jit(solution)/shard_map/row_panel/all_to_all | solution.py:271
  111.1 1.4 %copy-start = (f32[768,768]{1,0:T(8,128)}, f32[768,768]{1,0:T(8,128)S(1)}, u32[]{:S(2)}) copy-start(f32[768,768]{1,0:T(8,128)S(1)} %pivot_inverse.1.inverse_hbm) | copy-start | bytes 7077892
Sparse Core Ops, SparseCore 0:
  26.3 64.9 all-gather.1

commit v8 on v7

--- a/solution.py
+++ b/solution.py
@@ -103,8 +103,6 @@
     unit = jnp.where(unit, 1.0, 0.0)
     start = slice(TILE * first, TILE * first + TILE)
     diagonal_ref[...] = out_ref[start, start]
-    left_ref[...] = jnp.zeros(left_ref.shape, BF16)
-    right_ref[...] = jnp.zeros(right_ref.shape, BF16)
 
     def apply_last():
         wide = 2 * TILE
@@ -112,9 +110,10 @@
             here = slice(wide * c, wide * c + wide)
             out_ref[:, here] = out_ref[:, here] - product(left_ref[...], right_ref[:, here])
 
-    def step(k, carry):
+    def step(k, carry, pending=True):
         here = pl.ds(pl.multiple_of(k * TILE, TILE), TILE)
-        apply_last()
+        if pending:
+            apply_last()
         block = diagonal_ref[...]
         rows = invert_tile([block[8 * i : 8 * i + 8, :] for i in range(TILE // 8)])
         inverse = jnp.concatenate(rows, axis=0)
@@ -130,7 +129,8 @@
         diagonal_ref[...] = out_ref[after, after] - product(left_ref[after, :], right_ref[:, after])
         return carry
 
-    lax.fori_loop(first, last, step, 0)
+    step(jnp.int32(first), 0, pending=False)
+    lax.fori_loop(first + 1, last, step, 0)
     apply_last()
 
 
@@ -236,7 +236,7 @@
         out_specs=pl.BlockSpec(memory_space=pltpu.VMEM),
         scratch_shapes=[pltpu.VMEM(array.shape, F32) for array in arrays]
         + [pltpu.SemaphoreType.DMA((len(arrays),))],
-        compiler_params=pltpu.CompilerParams(vmem_limit_bytes=56 * 1024 * 1024),
+        compiler_params=pltpu.CompilerParams(vmem_limit_bytes=52 * 1024 * 1024),
         cost_estimate=pl.CostEstimate(flops=flops, bytes_accessed=8, transcendentals=0),
         name=name,
     )(place, *arrays)

time: 133 us -> 131 us (0.985)
  Pallas kernels: 52 us -> 50 us
where the time goes in v8:
time: 131 us; the launch traced here: 130 us
  Pallas kernels  50 us (38%)
  starting transfers between devices  25.4 us (19%)
  blocking collectives  21.7 us (17%)
  waiting for transfers between devices  13.5 us (10%)
  between operations  13.5 us (10%)
  local copies, waits for them, and re-layouts  5.53 us (4%)
    pallas_call x1, Pallas kernels, pivot_inverse(): pl.pallas_call(inverse_kernel, out_shape=jax.ShapeDtypeStruct((order, ord...  37.7 us
    all_to_all x1, blocking collectives, body(): lax.all_to_all(jnp.broadcast_to(pivot, (chips, band, K * B)), ('x', 'y'),...  21.7 us
    all_to_all x1, starting transfers between devices, body(): lax.all_to_all(jnp.broadcast_to(padded, (depth, band, TILE)), 'z', 0, 0)  14.7 us
    all_to_all x1, waiting for transfers between devices, body(): lax.all_to_all(jnp.broadcast_to(padded, (depth, band, TILE)), 'z', 0, 0)  13.4 us
    pallas_call x2, Pallas kernels, loading_call(): pl.pallas_call(functools.partial(kernel, band=band), out_shape=jax.ShapeD...  12.3 us
    all_to_all x1, starting transfers between devices, body(): row = lax.all_to_all(spread, ('x', 'y', 'c'), 0, 0)  6.29 us
    ppermute x1, starting transfers between devices, body(): other = lax.ppermute(own, 'c', [(0, 1), (1, 0)])  4.44 us
  transfers between devices with their start and end apart: 4, of which 1 were waited for; matrix products, arithmetic and copies ran while one was open for 2% of the time, Pallas kernels for 34%

profile of v8, /device:TPU:39, one launch (start us, length us, event | category | flops | bytes accessed | tf_op | source)
XLA Modules:
  0.0 130.4 jit_solution(17686298009202663927)
XLA Ops:
  6.5 0.0 slice-start
  6.5 1.2 fusion.3
  7.7 0.1 copy.13
  7.8 0.1 copy.12
  7.9 0.1 copy.14
  8.0 0.7 broadcast_in_dim.10
  8.7 14.7 %all-to-all-start = ((f32[16,24,128]{2,1,0:T(8,128)}), f32[16,24,128]{2,1,0:T(8,128)S(1)}, u32[]{:S(2)}, u32[]{:S(2)}) async-start(f32[16,24,128]{2,1,0:T(8,128)} %broadcast_in_dim.10), calls=%async_computation | async-start | bytes 393216 | tf_op jit(solution)/shard_map/pivot_z/all_to_all | solution.py:259
  23.4 0.0 all-gather.2.cloned.1.call-start
  23.4 0.6 fusion
  24.1 0.0 slice-done
  24.1 1.7 %broadcast_in_dim.9 = f32[32,24,800]{2,1,0:T(8,128)} broadcast(f32[24,800]{1,0:T(8,128)S(1)} %slice-done), dimensions={1,2} | broadcast | bytes 2534400 | tf_op jit(solution)/shard_map/broadcast_in_dim | solution.py:263
  25.8 0.0 all-gather.2.cloned.1.call-update
  25.8 13.4 %all-to-all-done = f32[16,24,128]{2,1,0:T(8,128)S(1)} async-done(((f32[16,24,128]{2,1,0:T(8,128)}), f32[16,24,128]{2,1,0:T(8,128)S(1)}, u32[]{:S(2)}, u32[]{:S(2)}) %all-to-all-start) | async-done | bytes 196640 | tf_op jit(solution)/shard_map/pivot_z/all_to_all | solution.py:259
  39.3 0.1 reshape.23
  39.4 0.1 broadcast_in_dim.11
  39.5 21.7 %all_to_all.15.own_ref = f32[16,24,768]{2,1,0:T(8,128)S(1)} all-to-all(f32[16,24,768]{2,1,0:T(8,128)S(1)} %broadcast_in_dim.11), channel_id=1, replica_groups=mesh['x'=4,'y'=4,'c'=2,'z'=16] {'x','y'}, dimensions={0} | all-to-all | bytes 2359296 | tf_op jit(solution)/shard_map/pivot_xy/all_to_all | solution.py:262
  61.3 4.4 %collective-permute-start = (f32[16,24,768]{2,1,0:T(8,128)S(1)}, f32[16,24,768]{2,1,0:T(8,128)S(1)}, u32[]{:S(2)}, u32[]{:S(2)}) collective-permute-start(f32[16,24,768]{2,1,0:T(8,128)S(1)} %all_to_all.15.own_ref), channel_id=1, source_target_pairs={{0,16},{16,0},{1,17},{17,1},{2,18},{18,2},{3,19},{19,3},{4,20},{20... | collective-permute-start | bytes 3538952 | tf_op jit(solution)/shard_map/pivot_core/ppermute | solution.py:269
  65.7 6.3 %all-to-all-start.2 = ((f32[32,24,800]{2,1,0:T(8,128)}), f32[32,24,800]{2,1,0:T(8,128)}, u32[]{:S(2)}, u32[]{:S(2)}) async-start(f32[32,24,800]{2,1,0:T(8,128)} %broadcast_in_dim.9), calls=%async_computation.2 | async-start | bytes 5505024 | tf_op jit(solution)/shard_map/row_panel/all_to_all | solution.py:271
  72.0 0.1 pad_add_fusion.1.place_ref
  72.1 0.0 collective-permute-done.other_ref
  72.1 37.7 %pivot_inverse.1.inverse_hbm = f32[768,768]{1,0:T(8,128)S(1)} custom-call(s32[2,16]{1,0:T(2,128)S(1)} %pad_add_fusion.slot_ref, f32[16,24,768]{2,1,0:T(8,128)S(1)} %all_to_all.15.own_ref, f32[16,24,768]{2,1,0:T(8,128)S(1)} %collective-permute-done.other_ref), custom_call_target="tpu_custom_call" | custom-call | flops 1 | bytes 8 | tf_op jit(solution)/shard_map/pivot_inverse/pallas_call | solution.py:148
  109.8 0.0 copy-start
  109.8 1.4 %copy-done = f32[768,768]{1,0:T(8,128)} copy-done((f32[768,768]{1,0:T(8,128)}, f32[768,768]{1,0:T(8,128)S(1)}, u32[]{:S(2)}) %copy-start) | copy-done | bytes 2359320
  111.2 0.0 all-gather.2.cloned.1.call-done.column_hbm
  111.2 6.2 %scale.1.scaled_hbm = f32[400,768]{1,0:T(8,128)S(1)} custom-call(s32[2]{0:T(128)S(1)} %pad_add_fusion.1.place_ref, f32[768,768]{1,0:T(8,128)} %copy-done, f32[768,400]{1,0:T(8,128)} %all-gather.2.cloned.1.call-done.column_hbm), custom_call_target="tpu_custom_call" | custom-call | flops 24000000000 | bytes 8 | tf_op jit(solution)/shard_map/scale/pallas_call | solution.py:231
  117.4 0.0 all-to-all-done.2
  117.4 6.1 %trailing_update.1 = f32[400,800]{1,0:T(8,128)} custom-call(s32[2]{0:T(128)S(1)} %pad_add_fusion.1.place_ref, f32[768,800]{1,0:T(8,128)} %bitcast.4.row_hbm, f32[400,768]{1,0:T(8,128)S(1)} %scale.1.scaled_hbm, f32[400,800]{1,0:T(8,128)} %current_hbm.1), custom_call_target="tpu_custom_call" | custom-call | flops 1 | bytes 8 | tf_op jit(solution)/shard_map/trailing_update/pallas_call | solution.py:231
  (6 shorter events, 0.1 us)
Async XLA Ops:
  6.5 17.5 %slice-start = ((f32[400,800]{1,0:T(8,128)}), f32[24,800]{1,0:T(8,128)S(1)}, s32[]{:S(2)}) async-start(f32[400,800]{1,0:T(8,128)} %current_hbm.1), calls=%async_computation.4 | async-start | bytes 172032 | tf_op jit(solution)/shard_map/slice | solution.py:256
  8.7 30.5 %all-to-all-start = ((f32[16,24,128]{2,1,0:T(8,128)}), f32[16,24,128]{2,1,0:T(8,128)S(1)}, u32[]{:S(2)}, u32[]{:S(2)}) async-start(f32[16,24,128]{2,1,0:T(8,128)} %broadcast_in_dim.10), calls=%async_computation | async-start | bytes 393216 | tf_op jit(solution)/shard_map/pivot_z/all_to_all | solution.py:259
  23.4 87.9 %all-gather.2.cloned.1.call-start = ((), (), s32[]{:S(2)}) async-start(), calls=%async_computation.3 | async-start | bytes 1671168 | tf_op jit(solution)/shard_map/column_panel/all_gather | solution.py:266
  61.3 10.9 %collective-permute-start = (f32[16,24,768]{2,1,0:T(8,128)S(1)}, f32[16,24,768]{2,1,0:T(8,128)S(1)}, u32[]{:S(2)}, u32[]{:S(2)}) collective-permute-start(f32[16,24,768]{2,1,0:T(8,128)S(1)} %all_to_all.15.own_ref), channel_id=1, source_target_pairs={{0,16},{16,0},{1,17},{17,1},{2,18},{18,2},{3,19},{19,3},{4,20},{20... | collective-permute-start | bytes 3538952 | tf_op jit(solution)/shard_map/pivot_core/ppermute | solution.py:269
  65.7 51.7 %all-to-all-start.2 = ((f32[32,24,800]{2,1,0:T(8,128)}), f32[32,24,800]{2,1,0:T(8,128)}, u32[]{:S(2)}, u32[]{:S(2)}) async-start(f32[32,24,800]{2,1,0:T(8,128)} %broadcast_in_dim.9), calls=%async_computation.2 | async-start | bytes 5505024 | tf_op jit(solution)/shard_map/row_panel/all_to_all | solution.py:271
  109.8 1.4 %copy-start = (f32[768,768]{1,0:T(8,128)}, f32[768,768]{1,0:T(8,128)S(1)}, u32[]{:S(2)}) copy-start(f32[768,768]{1,0:T(8,128)S(1)} %pivot_inverse.1.inverse_hbm) | copy-start | bytes 7077892
Sparse Core Ops, SparseCore 0:
  26.3 64.8 all-gather.1
